TPU v7x, 512 devices: a whole 4x8x8 slice. The times are simulated.
512 devices in a mesh: ta: 8 (over y), gx: 8 (over z_hi, core), gy: 8 (over x, z_lo).
Axes of the slice: x: 4, y: 8, z: 8 (z_hi: 4, z_lo: 2; z = z_hi * 2 + z_lo), core: 2. Of those that a mesh axis runs over, the one named last changes fastest.
Arguments:
- velocity: float32 [3, 8, 128, 128, 256], P(None, 'ta', 'gx', 'gy'), may hold values from -6 to 6
- pressure: float32 [8, 128, 128, 256], P('ta', 'gx', 'gy'), may hold values from -6 to 6
- forcing: float32 [3, 8, 128, 128, 256], P(None, 'ta', 'gx', 'gy'), may hold values from -6 to 6
- source: float32 [8, 128, 128, 256], P('ta', 'gx', 'gy'), may hold values from -6 to 6
- viscosity: float32 [3, 128, 128, 256], P(None, 'gx', 'gy'), may hold values from 0.05 to 0.5
Outputs:
- new_velocity: float32 [3, 8, 128, 128, 256], P(None, 'ta', 'gx', 'gy')
- new_pressure: float32 [8, 128, 128, 256], P('ta', 'gx', 'gy')
All inputs are finite; a program needn't handle non-finite values.
Results may differ from a plain program's by a relative error of at most 0.00002.
Values sent between devices are 32-bit elements; how exact they have to be, the bound alone decides.
No kernel may reach another device: no remote copies, remote signals or barrier semaphores. Data moves between devices by JAX's collectives and lax.ppermute only.
A program may use at most 64 MiB of HBM per device.

v0:
```python
import jax
import jax.numpy as jnp
from jax import lax
from jax.sharding import PartitionSpec as P

inverse_step = 1.0
relax_factor = 1.5
damping = 0.8


def shifted(x, axis, by):
    length = lax.axis_size(axis)
    pairs = [(i, i + by) for i in range(length) if 0 <= i + by < length]
    return lax.ppermute(x, axis, pairs)


def extended(cells, sides, width):
    for axis, dim in sides:
        count = lax.axis_size(axis)
        head = lax.slice_in_dim(cells, 0, width, axis=dim)
        tail = lax.slice_in_dim(cells, cells.shape[dim] - width, cells.shape[dim], axis=dim)
        cells = jnp.concatenate(
            [
                lax.ppermute(tail, axis, [(i, (i + 1) % count) for i in range(count)]),
                cells,
                lax.ppermute(head, axis, [((i + 1) % count, i) for i in range(count)]),
            ],
            axis=dim,
        )
    return cells


def shifted_2(value, axis, steps):
    count = lax.axis_size(axis)
    pairs = [(source, (source + steps) % count) for source in range(count)]
    return lax.ppermute(value, axis, pairs)


def gradient(field):
    return jnp.stack(
        [
            jnp.roll(field, -1, -3) - field,
            jnp.roll(field, -1, -2) - field,
            jnp.roll(field, -1, -1) - field,
        ]
    )


def divergence(flux):
    return (
        flux[0]
        - jnp.roll(flux[0], 1, -3)
        + (flux[1] - jnp.roll(flux[1], 1, -2))
        + (flux[2] - jnp.roll(flux[2], 1, -1))
    )


def neighbours(field):
    total = jnp.roll(field, 1, -3) + jnp.roll(field, -1, -3)
    total = total + jnp.roll(field, 1, -2) + jnp.roll(field, -1, -2)
    return total + jnp.roll(field, 1, -1) + jnp.roll(field, -1, -1)


def diagonal_sum(coeff):
    return (
        coeff[0]
        + jnp.roll(coeff[0], 1, -3)
        + coeff[1]
        + jnp.roll(coeff[1], 1, -2)
        + coeff[2]
        + jnp.roll(coeff[2], 1, -1)
    )


def inner_part(field, margin):
    return field[..., margin : field.shape[-3] - margin, margin : field.shape[-2] - margin, :]


def split_fields(padded, slab_steps):
    first = 3 * slab_steps
    shape_rest = padded.shape[1:]
    flow = padded[:first].reshape((3, slab_steps) + shape_rest)
    press = padded[first : first + slab_steps]
    position = first + slab_steps
    drive = padded[position : position + first].reshape((3, slab_steps) + shape_rest)
    position = position + first
    source_pad = None
    visc = padded[position : position + 3][:, None]
    return (flow, press, drive, source_pad, visc)


def body(velocity, pressure, forcing, source, viscosity):
    slab_steps = velocity.shape[1]
    cells_x = velocity.shape[2]
    cells_y = velocity.shape[3]
    cells_z = velocity.shape[4]
    arrived = shifted(velocity[:, slab_steps - 1], "ta", 1)
    previous = jnp.concatenate([arrived[:, None], velocity[:, : slab_steps - 1]], axis=1)
    driven = forcing + inverse_step * previous
    flat_flow = velocity.reshape(3 * slab_steps, cells_x, cells_y, cells_z)
    flat_drive = driven.reshape(3 * slab_steps, cells_x, cells_y, cells_z)
    margin = 2
    stacked = jnp.concatenate([flat_flow, pressure, flat_drive, viscosity], axis=0)
    padded = extended(stacked, (("gx", 1), ("gy", 2)), margin)
    flow, press, drive, source_pad, visc = split_fields(padded, slab_steps)
    momentum = (
        drive - (inverse_step * flow + visc * (6.0 * flow - neighbours(flow))) - gradient(press)
    )
    coeff = 1.0 / (relax_factor * (inverse_step + 6.0 * visc))
    total = inner_part(diagonal_sum(coeff), margin)
    right = inner_part(divergence(coeff * momentum) + divergence(flow), margin) - source
    change = -damping * right / total
    coeff_inner = inner_part(coeff, 1)
    bordered = extended(change, (("gx", 1), ("gy", 2)), 1)
    applied = inner_part(divergence(coeff_inner * gradient(bordered)), 1)
    change = change - damping * (right - applied) / total
    upper_x = shifted_2(change[:, :1], "gx", -1)
    upper_y = shifted_2(change[:, :, :1], "gy", -1)
    step_x = jnp.concatenate([change[:, 1:], upper_x], axis=1) - change
    step_y = jnp.concatenate([change[:, :, 1:], upper_y], axis=2) - change
    step_z = jnp.roll(change, -1, -1) - change
    slopes = jnp.stack([step_x, step_y, step_z])
    correction = inner_part(coeff, margin) * (inner_part(momentum, margin) - slopes)
    return (velocity + correction, pressure + change)


def solution(mesh):
    placed = (
        P(None, "ta", "gx", "gy", None),
        P("ta", "gx", "gy", None),
        P(None, "ta", "gx", "gy", None),
        P("ta", "gx", "gy", None),
        P(None, "gx", "gy", None),
    )
    return jax.shard_map(
        body,
        mesh=mesh,
        in_specs=placed,
        out_specs=(P(None, "ta", "gx", "gy", None), P("ta", "gx", "gy", None)),
        check_vma=False,
    )
```

profile of v0, /device:TPU:102, one launch (start us, length us, event | category | flops | bytes accessed | tf_op | source)
XLA Modules:
  0.0 110.0 jit_solution(2137324358368431132)
XLA Ops:
  0.7 2.7 %collective-permute-start = (f32[3,16,16,256]{3,2,1,0:T(8,128)}, f32[3,16,16,256]{3,2,1,0:T(8,128)S(1)}, u32[]{:S(2)}, u32[]{:S(2)}) collective-permute-start(f32[3,16,16,256]{3,2,1,0:T(8,128)} %bitcast.81), channel_id=1, source_target_pairs={{0,64},{64,128},{128,192},{192,256},{256,320},{320,384},{384,448},... | collective-permute-start | bytes 2359304 | tf_op jit(solution)/shard_map/ppermute | solution.py:14
  3.4 20.0 %collective-permute-done = f32[3,16,16,256]{3,2,1,0:T(8,128)S(1)} collective-permute-done((f32[3,16,16,256]{3,2,1,0:T(8,128)}, f32[3,16,16,256]{3,2,1,0:T(8,128)S(1)}, u32[]{:S(2)}, u32[]{:S(2)}) %collective-permute-start) | collective-permute-done | bytes 786464 | tf_op jit(solution)/shard_map/ppermute | solution.py:14
  23.4 1.3 %fusion.11 = f32[3,16,16,256]{3,2,1,0:T(8,128)S(1)} fusion(f32[3,16,16,256]{3,2,1,0:T(8,128)S(1)} %collective-permute-done, f32[3,1,16,16,256]{4,3,2,1,0:T(8,128)} %param.7), kind=kLoop, calls=%fused_computation.26 | loop fusion | flops 196608 | bytes 2359296 | tf_op jit(solution)/shard_map/reshape | solution.py:101
  24.8 1.9 %collective-permute-start.1 = (f32[10,2,16,256]{3,2,1,0:T(8,128)S(1)}, f32[10,2,16,256]{3,2,1,0:T(8,128)S(1)}, u32[]{:S(2)}, u32[]{:S(2)}) collective-permute-start(f32[10,2,16,256]{3,2,1,0:T(8,128)S(1)} %get-tuple-element.31), channel_id=1, source_target_pairs={{0,8},{8,16},{16,24},{24,32},{32,40},{40,48},{48,56},{56,0},{1,9},... | collective-permute-start | bytes 983048 | tf_op jit(solution)/shard_map/ppermute | solution.py:24
  26.7 8.6 %collective-permute-start.2 = (f32[10,2,16,256]{3,2,1,0:T(8,128)S(1)}, f32[10,2,16,256]{3,2,1,0:T(8,128)S(1)}, u32[]{:S(2)}, u32[]{:S(2)}) collective-permute-start(f32[10,2,16,256]{3,2,1,0:T(8,128)S(1)} %get-tuple-element.32), channel_id=1, source_target_pairs={{8,0},{16,8},{24,16},{32,24},{40,32},{48,40},{56,48},{0,56},{9,1},... | collective-permute-start | bytes 983048 | tf_op jit(solution)/shard_map/ppermute | solution.py:26
  35.3 6.3 %collective-permute-done.1 = f32[10,2,16,256]{3,2,1,0:T(8,128)S(1)} collective-permute-done((f32[10,2,16,256]{3,2,1,0:T(8,128)S(1)}, f32[10,2,16,256]{3,2,1,0:T(8,128)S(1)}, u32[]{:S(2)}, u32[]{:S(2)}) %collective-permute-start.1) | collective-permute-done | bytes 327712 | tf_op jit(solution)/shard_map/ppermute | solution.py:24
  41.9 4.2 %collective-permute-start.3 = (f32[10,20,2,256]{3,2,1,0:T(2,128)S(1)}, f32[10,20,2,256]{3,2,1,0:T(2,128)S(1)}, u32[]{:S(2)}, u32[]{:S(2)}) collective-permute-start(f32[10,20,2,256]{3,2,1,0:T(2,128)S(1)} %get-tuple-element.29), channel_id=1, source_target_pairs={{0,1},{1,2},{2,3},{3,4},{4,5},{5,6},{6,7},{7,0},{8,9},{9,10},{10,1... | collective-permute-start | bytes 1228808 | tf_op jit(solution)/shard_map/ppermute | solution.py:24
  46.1 2.0 %collective-permute-start.4 = (f32[10,20,2,256]{3,2,1,0:T(2,128)S(1)}, f32[10,20,2,256]{3,2,1,0:T(2,128)S(1)}, u32[]{:S(2)}, u32[]{:S(2)}) collective-permute-start(f32[10,20,2,256]{3,2,1,0:T(2,128)S(1)} %get-tuple-element.30), channel_id=1, source_target_pairs={{1,0},{2,1},{3,2},{4,3},{5,4},{6,5},{7,6},{0,7},{9,8},{10,9},{11,1... | collective-permute-start | bytes 1228808 | tf_op jit(solution)/shard_map/ppermute | solution.py:26
  48.1 8.4 %collective-permute-done.3 = f32[10,20,2,256]{3,2,1,0:T(2,128)S(1)} collective-permute-done((f32[10,20,2,256]{3,2,1,0:T(2,128)S(1)}, f32[10,20,2,256]{3,2,1,0:T(2,128)S(1)}, u32[]{:S(2)}, u32[]{:S(2)}) %collective-permute-start.3) | collective-permute-done | bytes 409632 | tf_op jit(solution)/shard_map/ppermute | solution.py:24
  56.5 7.6 %collective-permute-done.4 = f32[10,20,2,256]{3,2,1,0:T(2,128)S(1)} collective-permute-done((f32[10,20,2,256]{3,2,1,0:T(2,128)S(1)}, f32[10,20,2,256]{3,2,1,0:T(2,128)S(1)}, u32[]{:S(2)}, u32[]{:S(2)}) %collective-permute-start.4) | collective-permute-done | bytes 409632 | tf_op jit(solution)/shard_map/ppermute | solution.py:26
  64.0 1.2 %pad_maximum_fusion = f32[10,20,20,256]{3,2,1,0:T(8,128)S(1)} fusion(f32[10,20,2,256]{3,2,1,0:T(2,128)S(1)} %collective-permute-done.4, f32[10,2,16,256]{3,2,1,0:T(8,128)S(1)} %collective-permute-done.2, f32[3,16,16,256]{3,2,1,0:T(8,128)S(1)} %copy-done.1, f32[3,16,16,256]{3,2,1,0:T(8,128)S(1)} %fusion.11, f32[1,16,16,256]{3,2,1,0:T(8,128)S(1)} %copy-done.2, ...), kind=kLoop, calls=%fused_computation | loop fusion | flops 7168000 | bytes 8192000 | tf_op jit(solution)/shard_map/concatenate | solution.py:22
  67.8 2.2 %fusion.30 = (f32[3,20,20,256]{3,2,1,0:T(8,128)S(1)}, f32[3,20,20,256]{3,2,1,0:T(8,128)S(1)}, f32[3,20,20,256]{3,2,1,0:T(8,128)S(1)}) fusion(f32[10,20,20,256]{3,2,1,0:T(8,128)S(1)} %pad_maximum_fusion, f32[1,20,20,256]{3,2,1,0:T(8,128)S(1)} %get-tuple-element.12, f32[1,20,20,256]{3,2,1,0:T(8,128)S(1)} %get-tuple-element.11, ...), kind=kLoop, calls=%fused_computation.106 | loop fusion | flops 7372800 | bytes 15974400 | tf_op jit(solution)/shard_map/mul | solution.py:111
  71.5 0.9 multiply_divide_fusion.1
  72.5 1.9 %collective-permute-start.5 = (f32[1,1,16,256]{3,2,1,0:T(8,128)S(1)}, f32[1,1,16,256]{3,2,1,0:T(8,128)S(1)}, u32[]{:S(2)}, u32[]{:S(2)}) collective-permute-start(f32[1,1,16,256]{3,2,1,0:T(8,128)S(1)} %get-tuple-element.64), channel_id=1, source_target_pairs={{0,8},{8,16},{16,24},{24,32},{32,40},{40,48},{48,56},{56,0},{1,9},... | collective-permute-start | bytes 49160 | tf_op jit(solution)/shard_map/ppermute | solution.py:24
  74.4 5.8 %collective-permute-start.6 = (f32[1,1,16,256]{3,2,1,0:T(8,128)S(1)}, f32[1,1,16,256]{3,2,1,0:T(8,128)S(1)}, u32[]{:S(2)}, u32[]{:S(2)}) collective-permute-start(f32[1,1,16,256]{3,2,1,0:T(8,128)S(1)} %get-tuple-element.65), channel_id=1, source_target_pairs={{8,0},{16,8},{24,16},{32,24},{40,32},{48,40},{56,48},{0,56},{9,1},... | collective-permute-start | bytes 49160 | tf_op jit(solution)/shard_map/ppermute | solution.py:26
  80.2 1.4 %collective-permute-done.6 = f32[1,1,16,256]{3,2,1,0:T(8,128)S(1)} collective-permute-done((f32[1,1,16,256]{3,2,1,0:T(8,128)S(1)}, f32[1,1,16,256]{3,2,1,0:T(8,128)S(1)}, u32[]{:S(2)}, u32[]{:S(2)}) %collective-permute-start.6) | collective-permute-done | bytes 16416 | tf_op jit(solution)/shard_map/ppermute | solution.py:26
  81.7 4.9 %collective-permute-start.7 = (f32[1,18,1,256]{3,2,1,0:T(1,128)S(1)}, f32[1,18,1,256]{3,2,1,0:T(1,128)S(1)}, u32[]{:S(2)}, u32[]{:S(2)}) collective-permute-start(f32[1,18,1,256]{3,2,1,0:T(1,128)S(1)} %get-tuple-element.59), channel_id=1, source_target_pairs={{0,1},{1,2},{2,3},{3,4},{4,5},{5,6},{6,7},{7,0},{8,9},{9,10},{10,1... | collective-permute-start | bytes 55304 | tf_op jit(solution)/shard_map/ppermute | solution.py:24
  86.6 1.9 %collective-permute-start.8 = (f32[1,18,1,256]{3,2,1,0:T(1,128)S(1)}, f32[1,18,1,256]{3,2,1,0:T(1,128)S(1)}, u32[]{:S(2)}, u32[]{:S(2)}) collective-permute-start(f32[1,18,1,256]{3,2,1,0:T(1,128)S(1)} %get-tuple-element.60), channel_id=1, source_target_pairs={{1,0},{2,1},{3,2},{4,3},{5,4},{6,5},{7,6},{0,7},{9,8},{10,9},{11,1... | collective-permute-start | bytes 55304 | tf_op jit(solution)/shard_map/ppermute | solution.py:26
  88.6 5.8 %collective-permute-done.8 = f32[1,18,1,256]{3,2,1,0:T(1,128)S(1)} collective-permute-done((f32[1,18,1,256]{3,2,1,0:T(1,128)S(1)}, f32[1,18,1,256]{3,2,1,0:T(1,128)S(1)}, u32[]{:S(2)}, u32[]{:S(2)}) %collective-permute-start.8) | collective-permute-done | bytes 18464 | tf_op jit(solution)/shard_map/ppermute | solution.py:26
  95.5 1.0 fusion.32
  96.5 4.3 %collective-permute-start.9 = (f32[1,1,16,256]{3,2,1,0:T(8,128)S(1)}, f32[1,1,16,256]{3,2,1,0:T(8,128)S(1)}, u32[]{:S(2)}, u32[]{:S(2)}) collective-permute-start(f32[1,1,16,256]{3,2,1,0:T(8,128)S(1)} %slice.500), channel_id=1, source_target_pairs={{0,56},{8,0},{16,8},{24,16},{32,24},{40,32},{48,40},{56,48},{1,57}... | collective-permute-start | bytes 49160 | tf_op jit(solution)/shard_map/ppermute | solution.py:36
  100.9 1.9 %collective-permute-start.10 = (f32[1,16,1,256]{3,2,1,0:T(1,128)S(1)}, f32[1,16,1,256]{3,2,1,0:T(1,128)S(1)}, u32[]{:S(2)}, u32[]{:S(2)}) collective-permute-start(f32[1,16,1,256]{3,2,1,0:T(1,128)S(1)} %slice.502), channel_id=1, source_target_pairs={{0,7},{1,0},{2,1},{3,2},{4,3},{5,4},{6,5},{7,6},{8,15},{9,8},{10,9... | collective-permute-start | bytes 49160 | tf_op jit(solution)/shard_map/ppermute | solution.py:36
  103.0 5.6 %collective-permute-done.10 = f32[1,16,1,256]{3,2,1,0:T(1,128)S(1)} collective-permute-done((f32[1,16,1,256]{3,2,1,0:T(1,128)S(1)}, f32[1,16,1,256]{3,2,1,0:T(1,128)S(1)}, u32[]{:S(2)}, u32[]{:S(2)}) %collective-permute-start.10) | collective-permute-done | bytes 16416 | tf_op jit(solution)/shard_map/ppermute | solution.py:36
  108.8 1.3 %fusion.10 = f32[3,1,16,16,256]{4,3,2,1,0:T(8,128)} fusion(f32[3,1,16,16,256]{4,3,2,1,0:T(8,128)S(1)} %copy-done, f32[3,1,20,20,256]{4,3,2,0,1:T(8,128)S(1)} %bitcast.86, f32[3,1,20,20,256]{4,3,2,1,0:T(8,128)S(1)} %get-tuple-element.26, f32[1,1,16,16,256]{4,3,2,1,0:T(8,128)S(1)} %get-tuple-element.62, f32[1,1,16,16,256]{4,3,2,1,0:T(8,128)S(1)} %get-tuple-element.63, ...), kind=kLoop, calls=%fused_computation.24 | loop fusion | flops 983040 | bytes 3932160 | tf_op jit(solution)/shard_map/add | solution.py:124
  (65 shorter events, 5.6 us)
Async XLA Ops:
  0.6 24.0 %copy-start = (f32[3,1,16,16,256]{4,3,2,1,0:T(8,128)S(1)}, f32[3,1,16,16,256]{4,3,2,1,0:T(8,128)}, u32[]{:S(2)}) copy-start(f32[3,1,16,16,256]{4,3,2,1,0:T(8,128)} %param.5) | copy-start | bytes 2359300
  0.6 24.0 %copy-start.2 = (f32[1,16,16,256]{3,2,1,0:T(8,128)S(1)}, f32[1,16,16,256]{3,2,1,0:T(8,128)}, u32[]{:S(2)}) copy-start(f32[1,16,16,256]{3,2,1,0:T(8,128)} %param.6) | copy-start | bytes 786436
  0.7 24.0 %copy-start.1 = (f32[3,16,16,256]{3,2,1,0:T(8,128)S(1)}, f32[3,16,16,256]{3,2,1,0:T(8,128)}, u32[]{:S(2)}) copy-start(f32[3,16,16,256]{3,2,1,0:T(8,128)} %param.9) | copy-start | bytes 2359300
  0.7 22.7 %collective-permute-start = (f32[3,16,16,256]{3,2,1,0:T(8,128)}, f32[3,16,16,256]{3,2,1,0:T(8,128)S(1)}, u32[]{:S(2)}, u32[]{:S(2)}) collective-permute-start(f32[3,16,16,256]{3,2,1,0:T(8,128)} %bitcast.81), channel_id=1, source_target_pairs={{0,64},{64,128},{128,192},{192,256},{256,320},{320,384},{384,448},... | collective-permute-start | bytes 2359304 | tf_op jit(solution)/shard_map/ppermute | solution.py:14
  24.8 16.9 %collective-permute-start.1 = (f32[10,2,16,256]{3,2,1,0:T(8,128)S(1)}, f32[10,2,16,256]{3,2,1,0:T(8,128)S(1)}, u32[]{:S(2)}, u32[]{:S(2)}) collective-permute-start(f32[10,2,16,256]{3,2,1,0:T(8,128)S(1)} %get-tuple-element.31), channel_id=1, source_target_pairs={{0,8},{8,16},{16,24},{24,32},{32,40},{40,48},{48,56},{56,0},{1,9},... | collective-permute-start | bytes 983048 | tf_op jit(solution)/shard_map/ppermute | solution.py:24
  26.7 14.9 %collective-permute-start.2 = (f32[10,2,16,256]{3,2,1,0:T(8,128)S(1)}, f32[10,2,16,256]{3,2,1,0:T(8,128)S(1)}, u32[]{:S(2)}, u32[]{:S(2)}) collective-permute-start(f32[10,2,16,256]{3,2,1,0:T(8,128)S(1)} %get-tuple-element.32), channel_id=1, source_target_pairs={{8,0},{16,8},{24,16},{32,24},{40,32},{48,40},{56,48},{0,56},{9,1},... | collective-permute-start | bytes 983048 | tf_op jit(solution)/shard_map/ppermute | solution.py:26
  41.9 14.6 %collective-permute-start.3 = (f32[10,20,2,256]{3,2,1,0:T(2,128)S(1)}, f32[10,20,2,256]{3,2,1,0:T(2,128)S(1)}, u32[]{:S(2)}, u32[]{:S(2)}) collective-permute-start(f32[10,20,2,256]{3,2,1,0:T(2,128)S(1)} %get-tuple-element.29), channel_id=1, source_target_pairs={{0,1},{1,2},{2,3},{3,4},{4,5},{5,6},{6,7},{7,0},{8,9},{9,10},{10,1... | collective-permute-start | bytes 1228808 | tf_op jit(solution)/shard_map/ppermute | solution.py:24
  46.1 18.0 %collective-permute-start.4 = (f32[10,20,2,256]{3,2,1,0:T(2,128)S(1)}, f32[10,20,2,256]{3,2,1,0:T(2,128)S(1)}, u32[]{:S(2)}, u32[]{:S(2)}) collective-permute-start(f32[10,20,2,256]{3,2,1,0:T(2,128)S(1)} %get-tuple-element.30), channel_id=1, source_target_pairs={{1,0},{2,1},{3,2},{4,3},{5,4},{6,5},{7,6},{0,7},{9,8},{10,9},{11,1... | collective-permute-start | bytes 1228808 | tf_op jit(solution)/shard_map/ppermute | solution.py:26
  70.6 1.0 copy-start.3
  72.5 7.7 %collective-permute-start.5 = (f32[1,1,16,256]{3,2,1,0:T(8,128)S(1)}, f32[1,1,16,256]{3,2,1,0:T(8,128)S(1)}, u32[]{:S(2)}, u32[]{:S(2)}) collective-permute-start(f32[1,1,16,256]{3,2,1,0:T(8,128)S(1)} %get-tuple-element.64), channel_id=1, source_target_pairs={{0,8},{8,16},{16,24},{24,32},{32,40},{40,48},{48,56},{56,0},{1,9},... | collective-permute-start | bytes 49160 | tf_op jit(solution)/shard_map/ppermute | solution.py:24
  74.4 7.2 %collective-permute-start.6 = (f32[1,1,16,256]{3,2,1,0:T(8,128)S(1)}, f32[1,1,16,256]{3,2,1,0:T(8,128)S(1)}, u32[]{:S(2)}, u32[]{:S(2)}) collective-permute-start(f32[1,1,16,256]{3,2,1,0:T(8,128)S(1)} %get-tuple-element.65), channel_id=1, source_target_pairs={{8,0},{16,8},{24,16},{32,24},{40,32},{48,40},{56,48},{0,56},{9,1},... | collective-permute-start | bytes 49160 | tf_op jit(solution)/shard_map/ppermute | solution.py:26
  81.7 6.9 %collective-permute-start.7 = (f32[1,18,1,256]{3,2,1,0:T(1,128)S(1)}, f32[1,18,1,256]{3,2,1,0:T(1,128)S(1)}, u32[]{:S(2)}, u32[]{:S(2)}) collective-permute-start(f32[1,18,1,256]{3,2,1,0:T(1,128)S(1)} %get-tuple-element.59), channel_id=1, source_target_pairs={{0,1},{1,2},{2,3},{3,4},{4,5},{5,6},{6,7},{7,0},{8,9},{9,10},{10,1... | collective-permute-start | bytes 55304 | tf_op jit(solution)/shard_map/ppermute | solution.py:24
  86.6 7.8 %collective-permute-start.8 = (f32[1,18,1,256]{3,2,1,0:T(1,128)S(1)}, f32[1,18,1,256]{3,2,1,0:T(1,128)S(1)}, u32[]{:S(2)}, u32[]{:S(2)}) collective-permute-start(f32[1,18,1,256]{3,2,1,0:T(1,128)S(1)} %get-tuple-element.60), channel_id=1, source_target_pairs={{1,0},{2,1},{3,2},{4,3},{5,4},{6,5},{7,6},{0,7},{9,8},{10,9},{11,1... | collective-permute-start | bytes 55304 | tf_op jit(solution)/shard_map/ppermute | solution.py:26
  96.5 6.5 %collective-permute-start.9 = (f32[1,1,16,256]{3,2,1,0:T(8,128)S(1)}, f32[1,1,16,256]{3,2,1,0:T(8,128)S(1)}, u32[]{:S(2)}, u32[]{:S(2)}) collective-permute-start(f32[1,1,16,256]{3,2,1,0:T(8,128)S(1)} %slice.500), channel_id=1, source_target_pairs={{0,56},{8,0},{16,8},{24,16},{32,24},{40,32},{48,40},{56,48},{1,57}... | collective-permute-start | bytes 49160 | tf_op jit(solution)/shard_map/ppermute | solution.py:36
  100.9 7.7 %collective-permute-start.10 = (f32[1,16,1,256]{3,2,1,0:T(1,128)S(1)}, f32[1,16,1,256]{3,2,1,0:T(1,128)S(1)}, u32[]{:S(2)}, u32[]{:S(2)}) collective-permute-start(f32[1,16,1,256]{3,2,1,0:T(1,128)S(1)} %slice.502), channel_id=1, source_target_pairs={{0,7},{1,0},{2,1},{3,2},{4,3},{5,4},{6,5},{7,6},{8,15},{9,8},{10,9... | collective-permute-start | bytes 49160 | tf_op jit(solution)/shard_map/ppermute | solution.py:36
where the time goes:
time: 111 us; the launch traced here: 110 us
  waiting for transfers between devices  55.1 us (50%)
  starting transfers between devices  40.2 us (36%)
  other arithmetic  9.67 us (9%)
  local copies, waits for them, and re-layouts  3.9 us (4%)
  between operations  1.19 us (1%)
    ppermute x1, waiting for transfers between devices, shifted(): return lax.ppermute(x, axis, pairs)  20 us
    ppermute x4, starting transfers between devices, extended(): lax.ppermute(head, axis, [((i + 1) % count, i) for i in range(count)])  18.3 us
    ppermute x4, waiting for transfers between devices, extended(): lax.ppermute(head, axis, [((i + 1) % count, i) for i in range(count)])  14.8 us
    ppermute x4, waiting for transfers between devices, extended(): lax.ppermute(tail, axis, [(i, (i + 1) % count) for i in range(count)])  14.7 us
    ppermute x4, starting transfers between devices, extended(): lax.ppermute(tail, axis, [(i, (i + 1) % count) for i in range(count)])  12.9 us
    ppermute x2, starting transfers between devices, shifted_2(): return lax.ppermute(value, axis, pairs)  6.23 us
    ppermute x2, waiting for transfers between devices, shifted_2(): return lax.ppermute(value, axis, pairs)  5.6 us
    ppermute x1, starting transfers between devices, shifted(): return lax.ppermute(x, axis, pairs)  2.72 us
  transfers between devices with their start and end apart: 11, of which 7 were waited for; matrix products, arithmetic and copies ran while one was open for 0% of the time, Pallas kernels for 0%

commit v1 on v0

v1 whole, which is shorter than its diff:
```python
import functools

import jax
import jax.numpy as jnp
from jax import lax
from jax.experimental import pallas as pl
from jax.experimental.pallas import tpu as pltpu
from jax.sharding import PartitionSpec as P

RELAX = 1.5
DAMPING = 0.8
EXT = 24


def odd_pairs(n):
    return [p for i in range(1, n, 2) for p in ((i, (i + 1) % n), ((i + 1) % n, i))]


def even_pairs(n):
    return [p for i in range(0, n, 2) for p in ((i, i + 1), (i + 1, i))]


def swap_odd(x, axis):
    return lax.ppermute(x, axis, odd_pairs(lax.axis_size(axis)))


def swap_even(x, axis):
    return lax.ppermute(x, axis, even_pairs(lax.axis_size(axis)))


def above_z(x):
    return pltpu.roll(x, x.shape[1] - 1, 1)


def below_z(x):
    return pltpu.roll(x, 1, 1)


def above_y(x):
    return pltpu.roll(x, x.shape[0] - 1, 0)


def below_y(x):
    return pltpu.roll(x, 1, 0)


def row_id(shape):
    return lax.broadcasted_iota(jnp.int32, shape, 0)


def coeff_of(visc):
    return 1.0 / (RELAX * (1.0 + 6.0 * visc))


def local_kernel(v, p, f, visc, flux, coeff):
    nx, ny = p.shape[0], p.shape[1]
    rows = row_id(p.shape[1:])
    first, last = rows == 0, rows == ny - 1
    for i in range(nx):
        pressure = p[i]
        slope_x = (p[i + 1] if i + 1 < nx else jnp.zeros_like(pressure)) - pressure
        slope_y = jnp.where(last, 0.0, above_y(pressure)) - pressure
        slope_z = above_z(pressure) - pressure
        for c, slope in enumerate((slope_x, slope_y, slope_z)):
            nu = visc[c, i]
            k = coeff_of(nu)
            flow = v[c, i]
            near = above_z(flow) + below_z(flow)
            near = near + jnp.where(last, 0.0, above_y(flow)) + jnp.where(first, 0.0, below_y(flow))
            if i > 0:
                near = near + v[c, i - 1]
            if i + 1 < nx:
                near = near + v[c, i + 1]
            coeff[c, i] = k
            flux[c, i] = k * (f[c, i] + nu * near - slope) + flow * (1.0 - 1.0 / RELAX)


def edge_kernel(
    parity, flux0, coeff, prev, s, v_lo_x, v_hi_x, v_lo_y, v_hi_y,
    flux, part, scale, send_odd, send_even,
):
    nx, ny = s.shape[0], s.shape[1]
    shape = s.shape[1:]
    rows = row_id(shape)
    first, last = rows == 0, rows == ny - 1
    even_y = parity[1] == 0
    zero = jnp.zeros((1, shape[1]), jnp.float32)

    def send(layer, i, up, down):
        send_even[layer, i : i + 1, :] = jnp.where(even_y, up, down)
        send_odd[layer, i : i + 1, :] = jnp.where(even_y, down, up)

    for i in range(nx):
        own = []
        for c in range(3):
            k = coeff[c, i]
            a = (1.0 / RELAX - k) * (1.0 / 6.0)
            near = jnp.where(first, v_lo_y[c, i : i + 1, :], 0.0)
            near = near + jnp.where(last, v_hi_y[c, i : i + 1, :], 0.0)
            if i == 0:
                near = near + v_lo_x[c]
            if i == nx - 1:
                near = near + v_hi_x[c]
            value = flux0[c, i] + k * prev[c, i] + a * near
            if c == 0 and i == nx - 1:
                value = value - k * v_hi_x[3]
            if c == 1:
                value = value - k * jnp.where(last, v_hi_y[3, i : i + 1, :], 0.0)
            flux[c, i] = value
            own.append(value)
        right = own[0] + own[1] - jnp.where(first, 0.0, below_y(own[1])) + own[2] - below_z(own[2])
        right = right - s[i]
        kx, ky, kz = coeff[0, i], coeff[1, i], coeff[2, i]
        total = kx + ky + jnp.where(first, v_lo_y[3, i : i + 1, :], below_y(ky)) + kz + below_z(kz)
        if i > 0:
            right = right - flux[0, i - 1]
            total = total + coeff[0, i - 1]
        else:
            total = total + v_lo_x[3]
        over = -DAMPING / total
        part[i] = right
        scale[i] = over
        send(0, i, right[ny - 1 :, :], right[:1, :])
        send(1, i, own[1][ny - 1 :, :], right[1:2, :])
        send(2, i, over[ny - 1 :, :], over[:1, :])
        send(3, i, zero, over[1:2, :])
        if i == nx - 1:
            send(4, 0, own[0][ny - 1 :, :], own[0][:1, :])
            send(4, 1, zero, own[0][1:2, :])
            for j in range(2, nx):
                send(4, j, zero, zero)


def pick(even, odd_got, even_got, index):
    a, b = odd_got[index], even_got[index]
    return jnp.where(even, a, b), jnp.where(even, b, a)


def extend(dst, index, own, r16, r17, low):
    n = own.shape[0]
    dst[index, 0:n, :] = own
    dst[index, n : n + 1, :] = r16
    dst[index, n + 1 : n + 2, :] = r17
    dst[index, EXT - 1 : EXT, :] = low


def joined(i, even_y, got_odd, got_even, part, flux, right_x, scale_x, scale, index):
    ny = part.shape[1]
    row = slice(i, i + 1)
    lo0, hi0 = pick(even_y, got_odd, got_even, (0, row))
    lo1, hi1 = pick(even_y, got_odd, got_even, (1, row))
    lo2, hi2 = pick(even_y, got_odd, got_even, (2, row))
    _, hi3 = pick(even_y, got_odd, got_even, (3, row))
    own = part[i]
    own = own - jnp.where(row_id(own.shape) == 0, lo1, 0.0)
    extend(right_x, index, own, hi0 - flux[1, i, ny - 1 : ny, :], hi1, lo0)
    extend(scale_x, index, scale[i], hi2, hi3, lo2)


def side_strip(dst, index, even_y, got_odd, got_even, flux):
    nx = flux.shape[1]
    lo, hi = pick(even_y, got_odd, got_even, (4, slice(0, 1)))
    _, hi1 = pick(even_y, got_odd, got_even, (4, slice(1, 2)))
    extend(dst, index, flux[0, nx - 1], hi, hi1, lo)


def strip_kernel(
    parity, flux, part, scale, coeff, lo_y, hi_y, got_odd, got_even,
    send_odd, send_even, right_x, scale_x, side,
):
    nx, ny = part.shape[0], part.shape[1]
    even_x, even_y = parity[0] == 0, parity[1] == 0
    right_x[...] = jnp.zeros_like(right_x)
    scale_x[...] = jnp.zeros_like(scale_x)
    side[...] = jnp.zeros_like(side)
    for n, i in enumerate((0, 1, nx - 1)):
        joined(i, even_y, got_odd, got_even, part, flux, right_x, scale_x, scale, n)
    side_strip(side, 0, even_y, got_odd, got_even, flux)
    side[0, ny + 2 : ny + 3, :] = hi_y[4, nx - 1 : nx, :]
    scale_x[0, ny + 2 : ny + 3, :] = lo_y[3, 0:1, :]

    def send(layer, up, down):
        send_even[layer] = jnp.where(even_x, up, down)
        send_odd[layer] = jnp.where(even_x, down, up)

    send(0, right_x[2] * scale_x[2], right_x[1] * scale_x[1])
    send(1, side[0], right_x[0])
    send(2, jnp.zeros(side.shape[1:], jnp.float32), scale_x[0])


def last_kernel(
    parity, flux, part, scale, coeff, p, lo_x, hi_x, lo_y, hi_y,
    got_odd_y, got_even_y, got_odd_x, got_even_x,
    new_v, new_p, right_x, scale_x, side, first_c, kx, ky, kz,
):
    nx, ny = part.shape[0], part.shape[1]
    even_x, even_y = parity[0] == 0, parity[1] == 0
    right_x[...] = jnp.zeros_like(right_x)
    scale_x[...] = jnp.zeros_like(scale_x)
    lo0, hi0 = pick(even_x, got_odd_x, got_even_x, 0)
    lo1, hi1 = pick(even_x, got_odd_x, got_even_x, 1)
    _, hi2 = pick(even_x, got_odd_x, got_even_x, 2)
    side[...] = jnp.zeros_like(side)
    side_strip(side, 0, even_y, got_odd_y, got_even_y, flux)
    first_c[0] = lo0
    for i in range(nx):
        joined(i, even_y, got_odd_y, got_even_y, part, flux, right_x, scale_x, scale, i)
        right = right_x[i]
        if i == 0:
            right = right - lo1
        first_c[i + 1] = right * scale_x[i]
    first_c[nx + 1] = (hi1 - side[0]) * hi2
    first_c[nx + 2] = hi0
    scale_x[nx] = hi2
    zero = jnp.zeros((1, part.shape[2]), jnp.float32)
    extend(kx, 0, lo_x[3], lo1[ny + 2 : ny + 3, :], zero, zero)
    for i in range(nx):
        row = slice(i, i + 1)
        extend(kx, i + 1, coeff[0, i], hi_y[4, row, :], zero, zero)
        extend(ky, i, coeff[1, i], hi_y[5, row, :], zero, lo_y[3, row, :])
        extend(kz, i, coeff[2, i], hi_y[6, row, :], zero, zero)
    extend(kx, nx + 1, hi_x[4], zero, zero, zero)
    extend(ky, nx, hi_x[5], zero, zero, hi2[ny + 2 : ny + 3, :])
    extend(kz, nx, hi_x[6], zero, zero, zero)

    def sweep(i):
        mid = first_c[i + 1]
        gx = kx[i + 1] * (first_c[i + 2] - mid) - kx[i] * (mid - first_c[i])
        gy = ky[i] * (above_y(mid) - mid)
        gz = kz[i] * (above_z(mid) - mid)
        applied = gx + gy - below_y(gy) + gz - below_z(gz)
        return 2.0 * mid - scale_x[i] * applied

    now = sweep(0)
    for i in range(nx):
        after = sweep(i + 1)
        new_p[i] = p[i] + now[:ny]
        new_v[0, i] = flux[0, i] - coeff[0, i] * (after - now)[:ny]
        new_v[1, i] = flux[1, i] - coeff[1, i] * (above_y(now) - now)[:ny]
        new_v[2, i] = flux[2, i] - coeff[2, i] * (above_z(now) - now)[:ny]
        now = after


VM = pl.BlockSpec(memory_space=pltpu.VMEM)
SM = pl.BlockSpec(memory_space=pltpu.SMEM)


def call(kernel, args, outs, scratch=(), scalars=True):
    shapes = [jax.ShapeDtypeStruct(s, jnp.float32) for s in outs]
    size = sum(4 * a.size for a in args) + sum(4 * s.size for s in shapes)
    specs = [SM] + [VM] * (len(args) - 1) if scalars else [VM] * len(args)
    return pl.pallas_call(
        kernel,
        out_shape=shapes,
        in_specs=specs,
        out_specs=[VM] * len(shapes),
        scratch_shapes=[pltpu.VMEM(s, jnp.float32) for s in scratch],
        compiler_params=pltpu.CompilerParams(vmem_limit_bytes=40 * 2**20),
        cost_estimate=pl.CostEstimate(flops=size * 4, bytes_accessed=size, transcendentals=0),
    )(*args)


def faces(v, p, visc, dim):
    size = p.shape[dim]
    low = lambda x, d: lax.index_in_dim(x, 0, d, keepdims=False)
    top = lambda x, d: lax.index_in_dim(x, size - 1, d, keepdims=False)
    up = jnp.concatenate([top(v, dim + 1), coeff_of(top(visc[dim], dim))[None]], 0)
    up = jnp.concatenate([up, jnp.zeros((3,) + up.shape[1:], up.dtype)], 0)
    down = jnp.concatenate([low(v, dim + 1), low(p, dim)[None], coeff_of(low(visc, dim + 1))], 0)
    return up, down


def exchange(up, down, axis, even):
    odd_got = swap_odd(jnp.where(even, down, up), axis)
    even_got = swap_even(jnp.where(even, up, down), axis)
    return jnp.where(even, odd_got, even_got), jnp.where(even, even_got, odd_got)


def body(velocity, pressure, forcing, source, viscosity):
    v, p, f, s = velocity[:, 0], pressure[0], forcing[:, 0], source[0]
    nx, ny, nz = p.shape
    steps = lax.axis_size("ta")
    prev = lax.ppermute(v, "ta", [(i, i + 1) for i in range(steps - 1)])
    parity = jnp.stack([lax.axis_index("gx") % 2, lax.axis_index("gy") % 2]).astype(jnp.int32)
    even_x, even_y = parity[0] == 0, parity[1] == 0
    lo_y, hi_y = exchange(*faces(v, p, viscosity, 1), "gy", even_y)
    lo_x, hi_x = exchange(*faces(v, p, viscosity, 0), "gx", even_x)
    flux0, coeff = call(local_kernel, (v, p, f, viscosity), (v.shape, v.shape), scalars=False)
    flux, part, scale, send_odd, send_even = call(
        edge_kernel,
        (parity, flux0, coeff, prev, s, lo_x, hi_x, lo_y, hi_y),
        (v.shape, p.shape, p.shape, (5, nx, nz), (5, nx, nz)),
    )
    odd_y, even_y_got = swap_odd(send_odd, "gy"), swap_even(send_even, "gy")
    send_odd, send_even = call(
        strip_kernel,
        (parity, flux, part, scale, coeff, lo_y, hi_y, odd_y, even_y_got),
        ((3, EXT, nz), (3, EXT, nz)),
        ((3, EXT, nz), (3, EXT, nz), (1, EXT, nz)),
    )
    odd_x, even_x_got = swap_odd(send_odd, "gx"), swap_even(send_even, "gx")
    new_v, new_p = call(
        last_kernel,
        (parity, flux, part, scale, coeff, p, lo_x, hi_x, lo_y, hi_y, odd_y, even_y_got, odd_x, even_x_got),
        (v.shape, p.shape),
        (
            (nx, EXT, nz), (nx + 1, EXT, nz), (1, EXT, nz), (nx + 3, EXT, nz),
            (nx + 2, EXT, nz), (nx + 1, EXT, nz), (nx + 1, EXT, nz),
        ),
    )
    return new_v[:, None], new_p[None]


def solution(mesh):
    placed = (
        P(None, "ta", "gx", "gy", None),
        P("ta", "gx", "gy", None),
        P(None, "ta", "gx", "gy", None),
        P("ta", "gx", "gy", None),
        P(None, "gx", "gy", None),
    )
    return jax.shard_map(
        body,
        mesh=mesh,
        in_specs=placed,
        out_specs=(P(None, "ta", "gx", "gy", None), P("ta", "gx", "gy", None)),
        check_vma=False,
    )
```

time: 111 us -> 60.1 us (0.54)
  the two profiles are of different devices: /device:TPU:102 before, /device:TPU:24 now
where the time goes in v1:
time: 60.1 us; the launch traced here: 59.6 us
  starting transfers between devices  36.7 us (61%)
  waiting for transfers between devices  9.9 us (16%)
  local copies, waits for them, and re-layouts  6.93 us (12%)
  Pallas kernels  4.79 us (8%)
  between operations  0.96 us (2%)
    ppermute x4, starting transfers between devices, swap_odd(): return lax.ppermute(x, axis, odd_pairs(lax.axis_size(axis)))  21.8 us
    ppermute x4, starting transfers between devices, swap_even(): return lax.ppermute(x, axis, even_pairs(lax.axis_size(axis)))  10.2 us
    ppermute x4, waiting for transfers between devices, swap_odd(): return lax.ppermute(x, axis, odd_pairs(lax.axis_size(axis)))  8.69 us
    pallas_call x4, Pallas kernels, call(): pl.pallas_call(kernel, out_shape=shapes, in_specs=specs, out_specs=[VM] *...  4.79 us
    ppermute x1, starting transfers between devices, body(): prev = lax.ppermute(v, 'ta', [(i, i + 1) for i in range(steps - 1)])  4.68 us
    unnamed x15, local copies, waits for them, and re-layouts  2.53 us
    slice x2, local copies, waits for them, and re-layouts, faces(): low = lambda x, d: lax.index_in_dim(x, 0, d, keepdims=False)  1.26 us
    ppermute x1, local copies, waits for them, and re-layouts, body(): prev = lax.ppermute(v, 'ta', [(i, i + 1) for i in range(steps - 1)])  1.23 us
  transfers between devices with their start and end apart: 9, of which 4 were waited for; matrix products, arithmetic and copies ran while one was open for 5% of the time, Pallas kernels for 1%

profile of v1, /device:TPU:24, one launch (start us, length us, event | category | flops | bytes accessed | tf_op | source)
XLA Modules:
  0.0 59.6 jit_solution(8959464964838432114)
XLA Ops:
  0.7 2.2 %copy.50 = f32[3,1,16,16,256]{4,3,0,2,1:T(8,128)} copy(f32[3,1,16,16,256]{4,3,2,1,0:T(8,128)} %param.5) | data formatting | bytes 1572864 | tf_op args[0]
  2.8 4.7 %collective-permute-start = (f32[3,16,16,256]{3,2,0,1:T(8,128)}, f32[3,16,16,256]{3,2,0,1:T(8,128)}, u32[]{:S(2)}, u32[]{:S(2)}) collective-permute-start(f32[3,16,16,256]{3,2,0,1:T(8,128)} %bitcast.46), channel_id=1, source_target_pairs={{0,64},{64,128},{128,192},{192,256},{256,320},{320,384},{384,448},... | collective-permute-start | bytes 2359304 | tf_op jit(solution)/shard_map/ppermute | solution.py:283
  7.6 1.2 %fusion.16 = (f32[3,16,1,256]{3,2,0,1:T(1,128)S(1)}, f32[3,16,1,256]{3,2,0,1:T(1,128)S(1)}) fusion(f32[3,16,16,256]{3,2,0,1:T(8,128)} %bitcast.46), kind=kLoop, calls=%fused_computation.38 | loop fusion | bytes 196608 | tf_op jit(solution)/shard_map/slice | solution.py:265
  8.9 0.2 copy.52
  9.1 1.0 %slice-done = f32[1,16,16,256]{3,2,1,0:T(8,128)S(1)} async-done(((f32[3,16,16,256]{3,2,1,0:T(8,128)}), f32[1,16,16,256]{3,2,1,0:T(8,128)S(1)}, s32[]{:S(2)}) %slice-start) | async-done | bytes 262168 | tf_op jit(solution)/shard_map/slice | solution.py:267
  10.1 0.2 copy.51
  10.4 4.4 %collective-permute-start.4 = (f32[7,16,256]{2,1,0:T(8,128)S(1)}, f32[7,16,256]{2,1,0:T(8,128)S(1)}, u32[]{:S(2)}, u32[]{:S(2)}) collective-permute-start(f32[7,16,256]{2,1,0:T(8,128)S(1)} %get-tuple-element.36), channel_id=1, source_target_pairs={{0,1},{1,0},{2,3},{3,2},{4,5},{5,4},{6,7},{7,6},{8,9},{9,8},{10,11... | collective-permute-start | bytes 344072 | tf_op jit(solution)/shard_map/ppermute | solution.py:28
  14.9 4.1 %collective-permute-start.3 = (f32[7,16,256]{2,1,0:T(8,128)S(1)}, f32[7,16,256]{2,1,0:T(8,128)S(1)}, u32[]{:S(2)}, u32[]{:S(2)}) collective-permute-start(f32[7,16,256]{2,1,0:T(8,128)S(1)} %get-tuple-element.37), channel_id=1, source_target_pairs={{1,2},{2,1},{3,4},{4,3},{5,6},{6,5},{7,0},{0,7},{9,10},{10,9},{11,... | collective-permute-start | bytes 344072 | tf_op jit(solution)/shard_map/ppermute | solution.py:24
  19.0 0.8 %slice_bitcast_fusion.1 = (f32[3,16,256]{2,1,0:T(8,128)S(1)}, f32[3,16,256]{2,1,0:T(8,128)S(1)}) fusion(f32[3,16,16,256]{3,2,0,1:T(8,128)} %bitcast.46), kind=kLoop, calls=%fused_computation.16 | loop fusion | bytes 196608 | tf_op jit(solution)/shard_map/squeeze | solution.py:265
  20.0 1.9 %collective-permute-start.2 = (f32[7,16,256]{2,1,0:T(8,128)S(1)}, f32[7,16,256]{2,1,0:T(8,128)S(1)}, u32[]{:S(2)}, u32[]{:S(2)}) collective-permute-start(f32[7,16,256]{2,1,0:T(8,128)S(1)} %get-tuple-element.38), channel_id=1, source_target_pairs={{0,8},{8,0},{16,24},{24,16},{32,40},{40,32},{48,56},{56,48},{1,9},... | collective-permute-start | bytes 344072 | tf_op jit(solution)/shard_map/ppermute | solution.py:28
  21.9 10.7 %collective-permute-start.1 = (f32[7,16,256]{2,1,0:T(8,128)S(1)}, f32[7,16,256]{2,1,0:T(8,128)S(1)}, u32[]{:S(2)}, u32[]{:S(2)}) collective-permute-start(f32[7,16,256]{2,1,0:T(8,128)S(1)} %get-tuple-element.39), channel_id=1, source_target_pairs={{8,16},{16,8},{24,32},{32,24},{40,48},{48,40},{56,0},{0,56},{9,17}... | collective-permute-start | bytes 344072 | tf_op jit(solution)/shard_map/ppermute | solution.py:24
  32.6 0.8 %shard_map.68 = (f32[3,16,16,256]{3,2,1,0:T(8,128)S(1)}, f32[3,16,16,256]{3,2,1,0:T(8,128)S(1)}) custom-call(f32[3,16,16,256]{3,2,1,0:T(8,128)S(1)} %bitcast.49, f32[16,16,256]{2,1,0:T(8,128)S(1)} %bitcast.50, f32[3,16,16,256]{3,2,1,0:T(8,128)S(1)} %bitcast.52, f32[3,16,16,256]{3,2,1,0:T(8,128)S(1)} %copy-done.3), custom_call_target="tpu_custom_call" | custom-call | flops 16777216 | bytes 4194304 | tf_op jit(solution)/shard_map/pallas_call | solution.py:252
  33.5 2.8 %collective-permute-done.1 = f32[7,16,256]{2,1,0:T(8,128)S(1)} collective-permute-done((f32[7,16,256]{2,1,0:T(8,128)S(1)}, f32[7,16,256]{2,1,0:T(8,128)S(1)}, u32[]{:S(2)}, u32[]{:S(2)}) %collective-permute-start.1) | collective-permute-done | bytes 114720 | tf_op jit(solution)/shard_map/ppermute | solution.py:24
  36.3 1.2 %copy.28.prev = f32[3,16,16,256]{3,2,1,0:T(8,128)S(1)} copy(f32[3,16,16,256]{3,2,0,1:T(8,128)} %collective-permute-done) | data formatting | bytes 1572864 | tf_op jit(solution)/shard_map/ppermute | solution.py:283
  37.6 1.1 %shard_map.69 = (f32[3,16,16,256]{3,2,1,0:T(8,128)S(1)}, f32[16,16,256]{2,1,0:T(8,128)S(1)}, f32[16,16,256]{2,1,0:T(8,128)S(1)}, f32[5,16,256]{2,1,0:T(8,128)S(1)}, f32[5,16,256]{2,1,0:T(8,128)S(1)}) custom-call(s32[2]{0:T(128)S(1)} %pad_add_fusion.parity, f32[3,16,16,256]{3,2,1,0:T(8,128)S(1)} %get-tuple-element.13.flux0, ...), custom_call_target="tpu_custom_call" | custom-call | flops 18219040 | bytes 4554760 | tf_op jit(solution)/shard_map/pallas_call | solution.py:252
  38.7 3.3 %collective-permute-start.5 = (f32[5,16,256]{2,1,0:T(8,128)S(1)}, f32[5,16,256]{2,1,0:T(8,128)S(1)}, u32[]{:S(2)}, u32[]{:S(2)}) collective-permute-start(f32[5,16,256]{2,1,0:T(8,128)S(1)} %get-tuple-element.18), channel_id=1, source_target_pairs={{1,2},{2,1},{3,4},{4,3},{5,6},{6,5},{7,0},{0,7},{9,10},{10,9},{11,... | collective-permute-start | bytes 245768 | tf_op jit(solution)/shard_map/ppermute | solution.py:24
  42.0 1.9 %collective-permute-start.6 = (f32[5,16,256]{2,1,0:T(8,128)S(1)}, f32[5,16,256]{2,1,0:T(8,128)S(1)}, u32[]{:S(2)}, u32[]{:S(2)}) collective-permute-start(f32[5,16,256]{2,1,0:T(8,128)S(1)} %get-tuple-element.19), channel_id=1, source_target_pairs={{0,1},{1,0},{2,3},{3,2},{4,5},{5,4},{6,7},{7,6},{8,9},{9,8},{10,11... | collective-permute-start | bytes 245768 | tf_op jit(solution)/shard_map/ppermute | solution.py:28
  43.9 3.2 %collective-permute-done.5.got_odd.got_odd_y = f32[5,16,256]{2,1,0:T(8,128)S(1)} collective-permute-done((f32[5,16,256]{2,1,0:T(8,128)S(1)}, f32[5,16,256]{2,1,0:T(8,128)S(1)}, u32[]{:S(2)}, u32[]{:S(2)}) %collective-permute-start.5) | collective-permute-done | bytes 81952 | tf_op jit(solution)/shard_map/ppermute | solution.py:24
  47.1 1.2 %collective-permute-done.6.got_even.got_even_y = f32[5,16,256]{2,1,0:T(8,128)S(1)} collective-permute-done((f32[5,16,256]{2,1,0:T(8,128)S(1)}, f32[5,16,256]{2,1,0:T(8,128)S(1)}, u32[]{:S(2)}, u32[]{:S(2)}) %collective-permute-start.6) | collective-permute-done | bytes 81952 | tf_op jit(solution)/shard_map/ppermute | solution.py:28
  48.3 0.6 shard_map.70
  48.9 3.7 %collective-permute-start.7 = (f32[3,24,256]{2,1,0:T(8,128)S(1)}, f32[3,24,256]{2,1,0:T(8,128)S(1)}, u32[]{:S(2)}, u32[]{:S(2)}) collective-permute-start(f32[3,24,256]{2,1,0:T(8,128)S(1)} %get-tuple-element.20), channel_id=1, source_target_pairs={{8,16},{16,8},{24,32},{32,24},{40,48},{48,40},{56,0},{0,56},{9,17}... | collective-permute-start | bytes 221192 | tf_op jit(solution)/shard_map/ppermute | solution.py:24
  52.6 1.9 %collective-permute-start.8 = (f32[3,24,256]{2,1,0:T(8,128)S(1)}, f32[3,24,256]{2,1,0:T(8,128)S(1)}, u32[]{:S(2)}, u32[]{:S(2)}) collective-permute-start(f32[3,24,256]{2,1,0:T(8,128)S(1)} %get-tuple-element.21), channel_id=1, source_target_pairs={{0,8},{8,0},{16,24},{24,16},{32,40},{40,32},{48,56},{56,48},{1,9},... | collective-permute-start | bytes 221192 | tf_op jit(solution)/shard_map/ppermute | solution.py:28
  54.6 2.7 %collective-permute-done.7.got_odd_x = f32[3,24,256]{2,1,0:T(8,128)S(1)} collective-permute-done((f32[3,24,256]{2,1,0:T(8,128)S(1)}, f32[3,24,256]{2,1,0:T(8,128)S(1)}, u32[]{:S(2)}, u32[]{:S(2)}) %collective-permute-start.7) | collective-permute-done | bytes 73760 | tf_op jit(solution)/shard_map/ppermute | solution.py:24
  57.3 2.3 %shard_map.71 = (f32[3,16,16,256]{3,2,1,0:T(8,128)}, f32[16,16,256]{2,1,0:T(8,128)}) custom-call(s32[2]{0:T(128)S(1)} %pad_add_fusion.parity, f32[3,16,16,256]{3,2,1,0:T(8,128)S(1)} %get-tuple-element.15.flux, f32[16,16,256]{2,1,0:T(8,128)S(1)} %get-tuple-element.16.part, f32[16,16,256]{2,1,0:T(8,128)S(1)} %get-tuple-element.17.scale, ...), custom_call_target="tpu_custom_call" | custom-call | flops 16711712 | bytes 4177928 | tf_op jit(solution)/shard_map/pallas_call | solution.py:252
  (32 shorter events, 0.5 us)
Async XLA Ops:
  0.6 6.9 %copy-start.2 = (f32[3,16,16,256]{3,2,1,0:T(8,128)S(1)}, f32[3,16,16,256]{3,2,1,0:T(8,128)}, u32[]{:S(2)}) copy-start(f32[3,16,16,256]{3,2,1,0:T(8,128)} %visc.1) | copy-start | bytes 2359300
  0.6 31.9 %copy-start.4 = (f32[3,1,16,16,256]{4,3,2,1,0:T(8,128)S(1)}, f32[3,1,16,16,256]{4,3,2,1,0:T(8,128)}, u32[]{:S(2)}) copy-start(f32[3,1,16,16,256]{4,3,2,1,0:T(8,128)} %param.7) | copy-start | bytes 2359300
  2.8 33.5 %collective-permute-start = (f32[3,16,16,256]{3,2,0,1:T(8,128)}, f32[3,16,16,256]{3,2,0,1:T(8,128)}, u32[]{:S(2)}, u32[]{:S(2)}) collective-permute-start(f32[3,16,16,256]{3,2,0,1:T(8,128)} %bitcast.46), channel_id=1, source_target_pairs={{0,64},{64,128},{128,192},{192,256},{256,320},{320,384},{384,448},... | collective-permute-start | bytes 2359304 | tf_op jit(solution)/shard_map/ppermute | solution.py:283
  7.6 1.3 %copy-start.1 = (f32[1,16,16,256]{3,2,1,0:T(8,128)S(1)}, f32[1,16,16,256]{3,2,1,0:T(8,128)}, u32[]{:S(2)}) copy-start(f32[1,16,16,256]{3,2,1,0:T(8,128)} %param.6) | copy-start | bytes 786436
  8.9 1.2 %slice-start = ((f32[3,16,16,256]{3,2,1,0:T(8,128)}), f32[1,16,16,256]{3,2,1,0:T(8,128)S(1)}, s32[]{:S(2)}) async-start(f32[3,16,16,256]{3,2,1,0:T(8,128)} %visc.1), calls=%async_computation | async-start | bytes 524288 | tf_op jit(solution)/shard_map/slice | solution.py:267
  8.9 10.1 %copy-start.3 = (f32[3,16,16,256]{3,2,1,0:T(8,128)S(1)}, f32[3,16,16,256]{3,2,1,0:T(8,128)}, u32[]{:S(2)}) copy-start(f32[3,16,16,256]{3,2,1,0:T(8,128)} %visc.1) | copy-start | bytes 2359300
  10.2 22.4 %copy-start = (f32[3,1,16,16,256]{4,3,2,1,0:T(8,128)S(1)}, f32[3,1,16,16,256]{4,3,2,1,0:T(8,128)}, u32[]{:S(2)}) copy-start(f32[3,1,16,16,256]{4,3,2,1,0:T(8,128)} %param.5) | copy-start | bytes 2359300
  10.4 23.0 %collective-permute-start.4 = (f32[7,16,256]{2,1,0:T(8,128)S(1)}, f32[7,16,256]{2,1,0:T(8,128)S(1)}, u32[]{:S(2)}, u32[]{:S(2)}) collective-permute-start(f32[7,16,256]{2,1,0:T(8,128)S(1)} %get-tuple-element.36), channel_id=1, source_target_pairs={{0,1},{1,0},{2,3},{3,2},{4,5},{5,4},{6,7},{7,6},{8,9},{9,8},{10,11... | collective-permute-start | bytes 344072 | tf_op jit(solution)/shard_map/ppermute | solution.py:28
  14.9 18.6 %collective-permute-start.3 = (f32[7,16,256]{2,1,0:T(8,128)S(1)}, f32[7,16,256]{2,1,0:T(8,128)S(1)}, u32[]{:S(2)}, u32[]{:S(2)}) collective-permute-start(f32[7,16,256]{2,1,0:T(8,128)S(1)} %get-tuple-element.37), channel_id=1, source_target_pairs={{1,2},{2,1},{3,4},{4,3},{5,6},{6,5},{7,0},{0,7},{9,10},{10,9},{11,... | collective-permute-start | bytes 344072 | tf_op jit(solution)/shard_map/ppermute | solution.py:24
  20.0 13.5 %collective-permute-start.2 = (f32[7,16,256]{2,1,0:T(8,128)S(1)}, f32[7,16,256]{2,1,0:T(8,128)S(1)}, u32[]{:S(2)}, u32[]{:S(2)}) collective-permute-start(f32[7,16,256]{2,1,0:T(8,128)S(1)} %get-tuple-element.38), channel_id=1, source_target_pairs={{0,8},{8,0},{16,24},{24,16},{32,40},{40,32},{48,56},{56,48},{1,9},... | collective-permute-start | bytes 344072 | tf_op jit(solution)/shard_map/ppermute | solution.py:28
  21.9 14.4 %collective-permute-start.1 = (f32[7,16,256]{2,1,0:T(8,128)S(1)}, f32[7,16,256]{2,1,0:T(8,128)S(1)}, u32[]{:S(2)}, u32[]{:S(2)}) collective-permute-start(f32[7,16,256]{2,1,0:T(8,128)S(1)} %get-tuple-element.39), channel_id=1, source_target_pairs={{8,16},{16,8},{24,32},{32,24},{40,48},{48,40},{56,0},{0,56},{9,17}... | collective-permute-start | bytes 344072 | tf_op jit(solution)/shard_map/ppermute | solution.py:24
  36.3 1.3 %copy-start.5 = (f32[1,16,16,256]{3,2,1,0:T(8,128)S(1)}, f32[1,16,16,256]{3,2,1,0:T(8,128)}, u32[]{:S(2)}) copy-start(f32[1,16,16,256]{3,2,1,0:T(8,128)} %param.8) | copy-start | bytes 786436
  38.7 8.4 %collective-permute-start.5 = (f32[5,16,256]{2,1,0:T(8,128)S(1)}, f32[5,16,256]{2,1,0:T(8,128)S(1)}, u32[]{:S(2)}, u32[]{:S(2)}) collective-permute-start(f32[5,16,256]{2,1,0:T(8,128)S(1)} %get-tuple-element.18), channel_id=1, source_target_pairs={{1,2},{2,1},{3,4},{4,3},{5,6},{6,5},{7,0},{0,7},{9,10},{10,9},{11,... | collective-permute-start | bytes 245768 | tf_op jit(solution)/shard_map/ppermute | solution.py:24
  42.0 6.3 %collective-permute-start.6 = (f32[5,16,256]{2,1,0:T(8,128)S(1)}, f32[5,16,256]{2,1,0:T(8,128)S(1)}, u32[]{:S(2)}, u32[]{:S(2)}) collective-permute-start(f32[5,16,256]{2,1,0:T(8,128)S(1)} %get-tuple-element.19), channel_id=1, source_target_pairs={{0,1},{1,0},{2,3},{3,2},{4,5},{5,4},{6,7},{7,6},{8,9},{9,8},{10,11... | collective-permute-start | bytes 245768 | tf_op jit(solution)/shard_map/ppermute | solution.py:28
  48.9 8.4 %collective-permute-start.7 = (f32[3,24,256]{2,1,0:T(8,128)S(1)}, f32[3,24,256]{2,1,0:T(8,128)S(1)}, u32[]{:S(2)}, u32[]{:S(2)}) collective-permute-start(f32[3,24,256]{2,1,0:T(8,128)S(1)} %get-tuple-element.20), channel_id=1, source_target_pairs={{8,16},{16,8},{24,32},{32,24},{40,48},{48,40},{56,0},{0,56},{9,17}... | collective-permute-start | bytes 221192 | tf_op jit(solution)/shard_map/ppermute | solution.py:24
  52.6 4.6 %collective-permute-start.8 = (f32[3,24,256]{2,1,0:T(8,128)S(1)}, f32[3,24,256]{2,1,0:T(8,128)S(1)}, u32[]{:S(2)}, u32[]{:S(2)}) collective-permute-start(f32[3,24,256]{2,1,0:T(8,128)S(1)} %get-tuple-element.21), channel_id=1, source_target_pairs={{0,8},{8,0},{16,24},{24,16},{32,40},{40,32},{48,56},{56,48},{1,9},... | collective-permute-start | bytes 221192 | tf_op jit(solution)/shard_map/ppermute | solution.py:28

commit v2 on v1

v2 whole, which is shorter than its diff:
```python
import jax
import jax.numpy as jnp
from jax import lax
from jax.experimental import pallas as pl
from jax.experimental.pallas import tpu as pltpu
from jax.sharding import PartitionSpec as P

RELAX = 1.5
DAMPING = 0.8
EXT = 24


def odd_pairs(n):
    return [p for i in range(1, n, 2) for p in ((i, (i + 1) % n), ((i + 1) % n, i))]


def even_pairs(n):
    return [p for i in range(0, n, 2) for p in ((i, i + 1), (i + 1, i))]


def swap_odd(x, axis):
    return lax.ppermute(x, axis, odd_pairs(lax.axis_size(axis)))


def swap_even(x, axis):
    return lax.ppermute(x, axis, even_pairs(lax.axis_size(axis)))


def above_z(x):
    return pltpu.roll(x, x.shape[1] - 1, 1)


def below_z(x):
    return pltpu.roll(x, 1, 1)


def above_y(x):
    return pltpu.roll(x, x.shape[0] - 1, 0)


def below_y(x):
    return pltpu.roll(x, 1, 0)


def row_id(shape):
    return lax.broadcasted_iota(jnp.int32, shape, 0)


def coeff_of(visc):
    return 1.0 / (RELAX * (1.0 + 6.0 * visc))


def ring_plan(nx, ny):
    layers = [(c, i) for c in range(3) for i in (0, 1, nx - 1)] + [(0, nx - 2)]
    whole = {key: tile for tile, key in enumerate(layers)}
    lines = [(0, 1, ny - 1), (0, 1, ny - 2, ny - 1), (0, 1, ny - 1)]
    single = {}
    for c in range(3):
        for i in range(nx):
            if (c, i) not in whole:
                for j in lines[c]:
                    tile, row = divmod(len(single), ny)
                    single[c, i, j] = (len(whole) + tile, row)
    return whole, single, lines, len(whole) + -(-len(single) // ny)


def share(c):
    return (1.0 / RELAX - c) * (1.0 / 6.0)


def pick(even, odd_got, even_got, index):
    a, b = odd_got[index], even_got[index]
    return jnp.where(even, a, b), jnp.where(even, b, a)


def ring_kernel(v, ring):
    nx, ny = v.shape[1], v.shape[2]
    whole, single, _, tiles = ring_plan(nx, ny)
    ring[tiles - 1] = jnp.zeros(ring.shape[1:], jnp.float32)
    for (c, i), tile in whole.items():
        ring[tile] = v[c, i]
    for (c, i, j), (tile, row) in single.items():
        ring[tile, row : row + 1, :] = v[c, i, j : j + 1, :]


def face_kernel(parity, v, p, visc, send_odd, send_even):
    nx = v.shape[1]
    even_x = parity[0] == 0

    def send(layer, up, down):
        send_even[layer] = jnp.where(even_x, up, down)
        send_odd[layer] = jnp.where(even_x, down, up)

    for c in range(3):
        send(c, v[c, nx - 1], v[c, 0])
        send(4 + c, coeff_of(visc[c, nx - 1]), coeff_of(visc[c, 0]))
    send(3, jnp.zeros(p.shape[1:], jnp.float32), p[0])


def local_kernel(v, p, f, visc, ring, flux, coeff):
    nx, ny = p.shape[0], p.shape[1]
    rows = row_id(p.shape[1:])
    first, last = rows == 0, rows == ny - 1
    whole, single, lines, _ = ring_plan(nx, ny)
    for i in range(nx):
        pressure = p[i]
        slope_x = (p[i + 1] if i + 1 < nx else jnp.zeros_like(pressure)) - pressure
        slope_y = jnp.where(last, 0.0, above_y(pressure)) - pressure
        slope_z = above_z(pressure) - pressure
        for c, slope in enumerate((slope_x, slope_y, slope_z)):
            nu = visc[c, i]
            k = coeff_of(nu)
            flow = v[c, i]
            near = above_z(flow) + below_z(flow)
            near = near + jnp.where(last, 0.0, above_y(flow)) + jnp.where(first, 0.0, below_y(flow))
            if i > 0:
                near = near + v[c, i - 1]
            if i + 1 < nx:
                near = near + v[c, i + 1]
            coeff[c, i] = k
            if (c, i) in whole:
                prev = ring[whole[c, i]]
            else:
                prev = jnp.zeros(p.shape[1:], jnp.float32)
                for j in lines[c]:
                    tile, row = single[c, i, j]
                    prev = jnp.where(rows == j, ring[tile, row : row + 1, :], prev)
            flux[c, i] = k * (f[c, i] + prev + nu * near - slope) + flow * (1.0 - 1.0 / RELAX)


def edge_kernel(parity, flux0, coeff, v, p, s, got_odd, got_even, lo_x, hi_x, total, send_odd, send_even, own, inner):
    nx, ny = s.shape[0], s.shape[1]
    shape = s.shape[1:]
    rows = row_id(shape)
    first = rows == 0
    even_y = parity[1] == 0
    zero = jnp.zeros((1, shape[1]), jnp.float32)
    top, low, near = slice(ny - 1, ny), slice(0, 1), slice(1, 2)
    for layer in range(7):
        lo_x[layer], hi_x[layer] = pick(parity[0] == 0, got_odd, got_even, layer)

    def send(layer, i, up, down):
        send_even[layer, i : i + 1, :] = jnp.where(even_y, up, down)
        send_odd[layer, i : i + 1, :] = jnp.where(even_y, down, up)

    before = None
    for i in range(nx):
        row = slice(i, i + 1)
        flows = []
        for c in range(3):
            if 1 < i < nx - 1:
                inner[c, i - 2] = v[c, i]
            k = coeff[c, i]
            value = flux0[c, i]
            if i == 0:
                value = value + share(k) * lo_x[c]
            if i == nx - 1:
                value = value + share(k) * hi_x[c]
                if c == 0:
                    value = value - k * hi_x[3]
            flows.append(value)
        right = flows[0] + flows[1] - jnp.where(first, 0.0, below_y(flows[1])) + flows[2] - below_z(flows[2])
        right = right - s[i]
        kx, ky, kz = coeff[0, i], coeff[1, i], coeff[2, i]
        tot = kx + ky + jnp.where(first, 0.0, below_y(ky)) + kz + below_z(kz)
        if i > 0:
            right = right - before
            tot = tot + coeff[0, i - 1]
        else:
            tot = tot + lo_x[4]
        before = flows[0]
        total[i] = tot
        over = -DAMPING / tot
        for c in range(3):
            send(c, i, v[c, i, top, :], v[c, i, low, :])
            send(4 + c, i, coeff[c, i, top, :], coeff[c, i, low, :])
            own[c, row, :] = v[c, i, low, :]
            own[3 + c, row, :] = v[c, i, top, :]
        own[6, row, :] = p[i, low, :]
        own[7, row, :] = coeff[1, i, top, :]
        send(3, i, flows[1][top], p[i, low, :])
        send(7, i, right[top], right[low])
        send(8, i, over[top], right[near])
        send(9, i, zero, tot[low])
        send(10, i, zero, over[near])
    send(11, 0, before[top], before[low])
    send(11, 1, zero, before[near])
    for i in range(2, nx):
        send(11, i, zero, zero)


def extend(dst, index, own, r16, r17, low):
    n = own.shape[0]
    dst[index, 0:n, :] = own
    dst[index, n : n + 1, :] = r16
    dst[index, n + 1 : n + 2, :] = r17
    dst[index, EXT - 1 : EXT, :] = low


def whole_flux(c, i, flux0, coeff, prev, lo_x, hi_x, lo_y, hi_y, rows):
    nx, ny = flux0.shape[1], flux0.shape[2]
    first, last = rows == 0, rows == ny - 1
    row = slice(i, i + 1)
    k = coeff[c, i]
    near = jnp.where(first, lo_y[c, row, :], 0.0) + jnp.where(last, hi_y[c, row, :], 0.0)
    if i == 0:
        near = near + lo_x[c]
    if i == nx - 1:
        near = near + hi_x[c]
    value = flux0[c, i] + share(k) * near
    whole, _, lines, _ = ring_plan(nx, ny)
    if (c, i) not in whole:
        inside = (rows > 1) & (rows < ny - (2 if c == 1 else 1))
        value = value + k * jnp.where(inside, prev[c, i - 2], 0.0)
    if c == 0 and i == nx - 1:
        value = value - k * hi_x[3]
    if c == 1:
        value = value - k * jnp.where(last, hi_y[3, row, :], 0.0)
    return value


def whole_layer(i, flows, before, s, total, out_rows, lo_y, right_x, scale_x, index, first):
    ny = s.shape[1]
    row = slice(i, i + 1)
    right = flows[0] + flows[1] - jnp.where(first, out_rows[0, row, :], below_y(flows[1]))
    right = right + flows[2] - below_z(flows[2]) - s[i]
    if before is not None:
        right = right - before
    scale = -DAMPING / (total[i] + jnp.where(first, lo_y[5, row, :], 0.0))
    extend(
        right_x, index, right,
        out_rows[2, row, :] - flows[1][ny - 1 : ny], out_rows[3, row, :], out_rows[1, row, :],
    )
    extend(scale_x, index, scale, out_rows[4, row, :], out_rows[6, row, :], out_rows[5, row, :])


def strip_kernel(
    parity, flux0, coeff, s, total, lo_x, hi_x, got_odd, got_even, own,
    lo_y, hi_y, out_rows, send_odd, send_even, right_x, scale_x, side,
):
    nx, ny = s.shape[0], s.shape[1]
    even_x, even_y = parity[0] == 0, parity[1] == 0
    rows = row_id(s.shape[1:])
    first = rows == 0
    for layer in range(12):
        lo_y[layer], hi_y[layer] = pick(even_y, got_odd, got_even, layer)

    def along_x(x):
        return x - jnp.where(first_x, 0.0, pltpu.roll(x, 1, 0))

    first_x = row_id((nx, s.shape[2])) == 0
    edge = share(lo_y[4]) * own[0]
    push_y = share(lo_y[5]) * own[1] - lo_y[5] * own[6]
    push_z = share(lo_y[6]) * own[2]
    out_rows[0] = lo_y[3] + push_y
    out_rows[1] = lo_y[7] + along_x(edge) + push_y + push_z - below_z(push_z)
    out_rows[5] = lo_y[8]
    side_low = lo_y[11, 0:1, :] + edge[nx - 1 :]
    edge = share(hi_y[4]) * own[3]
    push_y = share(hi_y[5]) * own[4]
    push_z = share(hi_y[6]) * own[5]
    out_rows[2] = hi_y[7] + along_x(edge) + push_y + push_z - below_z(push_z)
    out_rows[3] = hi_y[8] - push_y
    out_rows[4] = -DAMPING / (hi_y[9] + own[7])
    out_rows[6] = hi_y[10]
    side_16, side_17 = hi_y[11, 0:1, :] + edge[nx - 1 :], hi_y[11, 1:2, :]

    right_x[...] = jnp.zeros_like(right_x)
    scale_x[...] = jnp.zeros_like(scale_x)
    side[...] = jnp.zeros_like(side)
    args = (flux0, coeff, None, lo_x, hi_x, lo_y, hi_y, rows)
    before = None
    for n, i in enumerate((0, 1, nx - 1)):
        if i == nx - 1:
            before = whole_flux(0, i - 1, *args)
        flows = [whole_flux(c, i, *args) for c in range(3)]
        whole_layer(i, flows, before, s, total, out_rows, lo_y, right_x, scale_x, n, first)
        before = flows[0]
    extend(side, 0, before, side_16, side_17, side_low)
    side[0, ny + 2 : ny + 3, :] = hi_y[4, nx - 1 : nx, :]
    scale_x[0, ny + 2 : ny + 3, :] = lo_y[5, 0:1, :]
    out_rows[7] = jnp.zeros(out_rows.shape[1:], jnp.float32)
    out_rows[7, 0:1, :] = side_low
    out_rows[7, 1:2, :] = side_16
    out_rows[7, 2:3, :] = side_17

    def send(layer, up, down):
        send_even[layer] = jnp.where(even_x, up, down)
        send_odd[layer] = jnp.where(even_x, down, up)

    send(0, right_x[2] * scale_x[2], right_x[1] * scale_x[1])
    send(1, side[0], right_x[0])
    send(2, jnp.zeros(side.shape[1:], jnp.float32), scale_x[0])


def own_kernel(
    flux0, coeff, prev, s, total, lo_x, hi_x, lo_y, hi_y, out_rows,
    flux, first_c, scale_x, side, kx, ky, kz,
):
    nx, ny = s.shape[0], s.shape[1]
    rows = row_id(s.shape[1:])
    first = rows == 0
    args = (flux0, coeff, prev, lo_x, hi_x, lo_y, hi_y, rows)
    zero = jnp.zeros((1, s.shape[2]), jnp.float32)
    for ref in (first_c, scale_x, side, kx, ky, kz):
        ref[...] = jnp.zeros_like(ref)
    before = None
    for i in range(nx):
        row = slice(i, i + 1)
        flows = [whole_flux(c, i, *args) for c in range(3)]
        for c in range(3):
            flux[c, i] = flows[c]
        whole_layer(i, flows, before, s, total, out_rows, lo_y, first_c, scale_x, i, first)
        first_c[i] = first_c[i] * scale_x[i]
        before = flows[0]
        extend(kx, i, coeff[0, i], hi_y[4, row, :], zero, zero)
        extend(ky, i, coeff[1, i], hi_y[5, row, :], zero, lo_y[5, row, :])
        extend(kz, i, coeff[2, i], hi_y[6, row, :], zero, zero)
    extend(side, 0, before, out_rows[7, 1:2, :], out_rows[7, 2:3, :], out_rows[7, 0:1, :])


def last_kernel(
    parity, flux, own_c, own_scale, side, own_kx, own_ky, own_kz, p, lo_x, hi_x, got_odd, got_even,
    new_v, new_p, edge,
):
    nx, ny = p.shape[0], p.shape[1]
    even_x = parity[0] == 0
    lo0, hi0 = pick(even_x, got_odd, got_even, 0)
    lo1, hi1 = pick(even_x, got_odd, got_even, 1)
    _, hi2 = pick(even_x, got_odd, got_even, 2)
    edge[...] = jnp.zeros_like(edge)
    edge[0, 0:ny, :] = lo_x[4]
    edge[0, ny : ny + 1, :] = lo1[ny + 2 : ny + 3, :]
    edge[1, 0:ny, :] = hi_x[4]
    edge[2, 0:ny, :] = hi_x[5]
    edge[2, EXT - 1 : EXT, :] = hi2[ny + 2 : ny + 3, :]
    edge[3, 0:ny, :] = hi_x[6]

    def first_c(i):
        if i == -1:
            return lo0
        if i == 0:
            return own_c[0] - lo1 * own_scale[0]
        if i == nx:
            return (hi1 - side[0]) * hi2
        if i == nx + 1:
            return hi0
        return own_c[i]

    def sweep(i, low, mid, high):
        if i < nx:
            kx, ky, kz, scale = own_kx[i], own_ky[i], own_kz[i], own_scale[i]
        else:
            kx, ky, kz, scale = edge[1], edge[2], edge[3], hi2
        below_kx = own_kx[i - 1] if i > 0 else edge[0]
        gx = kx * (high - mid) - below_kx * (mid - low)
        gy = ky * (above_y(mid) - mid)
        gz = kz * (above_z(mid) - mid)
        applied = gx + gy - below_y(gy) + gz - below_z(gz)
        return 2.0 * mid - scale * applied

    low, mid, high = first_c(-1), first_c(0), first_c(1)
    now = sweep(0, low, mid, high)
    for i in range(nx):
        low, mid, high = mid, high, first_c(i + 2)
        after = sweep(i + 1, low, mid, high)
        new_p[i] = p[i] + now[:ny]
        new_v[0, i] = flux[0, i] - own_kx[i, :ny] * (after - now)[:ny]
        new_v[1, i] = flux[1, i] - own_ky[i, :ny] * (above_y(now) - now)[:ny]
        new_v[2, i] = flux[2, i] - own_kz[i, :ny] * (above_z(now) - now)[:ny]
        now = after


VM = pl.BlockSpec(memory_space=pltpu.VMEM)
SM = pl.BlockSpec(memory_space=pltpu.SMEM)


def call(kernel, args, outs, scratch=(), scalars=True, flops=1000):
    shapes = [jax.ShapeDtypeStruct(s, jnp.float32) for s in outs]
    size = sum(4 * a.size for a in args) + sum(4 * s.size for s in shapes)
    specs = [SM] + [VM] * (len(args) - 1) if scalars else [VM] * len(args)
    return pl.pallas_call(
        kernel,
        out_shape=shapes,
        in_specs=specs,
        out_specs=[VM] * len(shapes),
        scratch_shapes=[pltpu.VMEM(s, jnp.float32) for s in scratch],
        compiler_params=pltpu.CompilerParams(vmem_limit_bytes=40 * 2**20),
        cost_estimate=pl.CostEstimate(flops=flops, bytes_accessed=size, transcendentals=0),
    )(*args)


def body(velocity, pressure, forcing, source, viscosity):
    v, p, f, s = velocity[:, 0], pressure[0], forcing[:, 0], source[0]
    nx, ny, nz = p.shape
    steps = lax.axis_size("ta")
    ahead = [(i, i + 1) for i in range(steps - 1)]
    parity = jnp.stack([lax.axis_index("gx") % 2, lax.axis_index("gy") % 2]).astype(jnp.int32)
    (ring,) = call(ring_kernel, (v,), ((ring_plan(nx, ny)[3], ny, nz),), scalars=False, flops=20_000_000_000)
    face_odd, face_even = call(face_kernel, (parity, v, p, viscosity), ((7, ny, nz), (7, ny, nz)), flops=20_000_000_000)
    odd_x, even_x = swap_odd(face_odd, "gx"), swap_even(face_even, "gx")
    ring = lax.ppermute(ring, "ta", ahead)
    flux0, coeff = call(local_kernel, (v, p, f, viscosity, ring), (v.shape,) * 2, scalars=False)
    lo_x, hi_x, total, send_odd, send_even, own, inner = call(
        edge_kernel,
        (parity, flux0, coeff, v, p, s, odd_x, even_x),
        ((7, ny, nz), (7, ny, nz), p.shape, (12, nx, nz), (12, nx, nz), (8, nx, nz), (3, nx - 3, ny, nz)),
    )
    prev = lax.ppermute(inner, "ta", ahead)
    odd_y, even_y = swap_odd(send_odd, "gy"), swap_even(send_even, "gy")
    lo_y, hi_y, out_rows, send_odd, send_even = call(
        strip_kernel,
        (parity, flux0, coeff, s, total, lo_x, hi_x, odd_y, even_y, own),
        ((12, nx, nz), (12, nx, nz), (8, nx, nz), (3, EXT, nz), (3, EXT, nz)),
        ((3, EXT, nz), (3, EXT, nz), (1, EXT, nz)),
        flops=20_000_000_000,
    )
    odd_x, even_x = swap_odd(send_odd, "gx"), swap_even(send_even, "gx")
    flux, first_c, scale, side, kx, ky, kz = call(
        own_kernel,
        (flux0, coeff, prev, s, total, lo_x, hi_x, lo_y, hi_y, out_rows),
        (v.shape, (nx, EXT, nz), (nx, EXT, nz), (1, EXT, nz)) + ((nx, EXT, nz),) * 3,
        scalars=False,
    )
    new_v, new_p = call(
        last_kernel,
        (parity, flux, first_c, scale, side, kx, ky, kz, p, lo_x, hi_x, odd_x, even_x),
        (v.shape, p.shape),
        ((4, EXT, nz),),
    )
    return new_v[:, None], new_p[None]


def solution(mesh):
    placed = (
        P(None, "ta", "gx", "gy", None),
        P("ta", "gx", "gy", None),
        P(None, "ta", "gx", "gy", None),
        P("ta", "gx", "gy", None),
        P(None, "gx", "gy", None),
    )
    return jax.shard_map(
        body,
        mesh=mesh,
        in_specs=placed,
        out_specs=(P(None, "ta", "gx", "gy", None), P("ta", "gx", "gy", None)),
        check_vma=False,
    )
```

time: 60.1 us -> 50.6 us (0.84)
  local copies, waits for them, and re-layouts: 6.93 us -> 1.15 us
  starting transfers between devices: 36.7 us -> 32.6 us
  Pallas kernels: 4.79 us -> 6.09 us
    ppermute x4 -> x3, waiting for transfers between devices: 8.69 us -> 1.89 us  [swap_odd(): return lax.ppermute(x, axis, odd_pairs(lax.axis_size(axis)))]
    ppermute x1 -> x2, waiting for transfers between devices: 0.01 us -> 5.02 us  [the longest x1 5.01 us: body(): prev = lax.ppermute(inner, 'ta', ahead)]
    ppermute x4 -> x3, starting transfers between devices: 10.2 us -> 5.76 us  [swap_even(): return lax.ppermute(x, axis, even_pairs(lax.axis_size(axis)))]
    ppermute x1 -> x2, starting transfers between devices: 4.68 us -> 7.41 us  [the longest x1 4.83 us: body(): ring = lax.ppermute(ring, 'ta', ahead)]
    ppermute x4 -> x3, starting transfers between devices: 21.8 us -> 19.5 us  [swap_odd(): return lax.ppermute(x, axis, odd_pairs(lax.axis_size(axis)))]
    slice x4 -> x0, local copies, waits for them, and re-layouts: 2.25 us -> none  [the longest x2 1.26 us: faces(): low = lambda x, d: lax.index_in_dim(x, 0, d, keepdims=False)]
    ppermute x4 -> x3, waiting for transfers between devices: 1.2 us -> 2.61 us  [swap_even(): return lax.ppermute(x, axis, even_pairs(lax.axis_size(axis)))]
    unnamed x15 -> x12, local copies, waits for them, and re-layouts: 2.53 us -> 1.15 us
  transfers between devices with their start and end apart: 9 -> 8, of which waited for: 4 -> 4; matrix products, arithmetic and copies ran while one was open for 5% -> 0% of each run, Pallas kernels for 1% -> 5%
where the time goes in v2:
time: 50.6 us; the launch traced here: 50.3 us
  starting transfers between devices  32.6 us (64%)
  waiting for transfers between devices  9.51 us (19%)
  Pallas kernels  6.09 us (12%)
  local copies, waits for them, and re-layouts  1.15 us (2%)
  between operations  0.81 us (2%)
    ppermute x3, starting transfers between devices, swap_odd(): return lax.ppermute(x, axis, odd_pairs(lax.axis_size(axis)))  19.5 us
    pallas_call x7, Pallas kernels, call(): pl.pallas_call(kernel, out_shape=shapes, in_specs=specs, out_specs=[VM] *...  6.09 us
    ppermute x3, starting transfers between devices, swap_even(): return lax.ppermute(x, axis, even_pairs(lax.axis_size(axis)))  5.76 us
    ppermute x1, waiting for transfers between devices, body(): prev = lax.ppermute(inner, 'ta', ahead)  5.01 us
    ppermute x1, starting transfers between devices, body(): ring = lax.ppermute(ring, 'ta', ahead)  4.83 us
    ppermute x3, waiting for transfers between devices, swap_even(): return lax.ppermute(x, axis, even_pairs(lax.axis_size(axis)))  2.61 us
    ppermute x1, starting transfers between devices, body(): prev = lax.ppermute(inner, 'ta', ahead)  2.59 us
    ppermute x3, waiting for transfers between devices, swap_odd(): return lax.ppermute(x, axis, odd_pairs(lax.axis_size(axis)))  1.89 us
  transfers between devices with their start and end apart: 8, of which 4 were waited for; matrix products, arithmetic and copies ran while one was open for 0% of the time, Pallas kernels for 5%

profile of v2, /device:TPU:24, one launch (start us, length us, event | category | flops | bytes accessed | tf_op | source)
XLA Modules:
  0.0 50.3 jit_solution(7353902066845836773)
XLA Ops:
  0.6 1.1 %copy-done = f32[3,1,16,16,256]{4,3,2,1,0:T(8,128)S(1)} copy-done((f32[3,1,16,16,256]{4,3,2,1,0:T(8,128)S(1)}, f32[3,1,16,16,256]{4,3,2,1,0:T(8,128)}, u32[]{:S(2)}) %copy-start) | copy-done | bytes 786456
  1.8 0.1 shard_map.68
  1.9 4.8 %collective-permute-start = (f32[18,16,256]{2,1,0:T(8,128)S(1)}, f32[18,16,256]{2,1,0:T(8,128)S(1)}, u32[]{:S(2)}, u32[]{:S(2)}) collective-permute-start(f32[18,16,256]{2,1,0:T(8,128)S(1)} %shard_map.68), channel_id=1, source_target_pairs={{0,64},{64,128},{128,192},{192,256},{256,320},{320,384},{384,448},... | collective-permute-start | bytes 884744 | tf_op jit(solution)/shard_map/ppermute | solution.py:402
  6.7 0.1 pad_add_fusion.parity
  6.8 0.6 %shard_map.70 = (f32[7,16,256]{2,1,0:T(8,128)S(1)}, f32[7,16,256]{2,1,0:T(8,128)S(1)}) custom-call(s32[2]{0:T(128)S(1)} %pad_add_fusion.parity, f32[3,16,16,256]{3,2,1,0:T(8,128)S(1)} %bitcast.11, f32[16,16,256]{2,1,0:T(8,128)S(1)} %bitcast.14, f32[3,16,16,256]{3,2,1,0:T(8,128)S(1)} %copy-done.5), custom_call_target="tpu_custom_call" | custom-call | flops 20000000000 | bytes 2064392 | tf_op jit(solution)/shard_map/pallas_call | solution.py:382
  7.4 10.1 %collective-permute-start.1 = (f32[7,16,256]{2,1,0:T(8,128)S(1)}, f32[7,16,256]{2,1,0:T(8,128)S(1)}, u32[]{:S(2)}, u32[]{:S(2)}) collective-permute-start(f32[7,16,256]{2,1,0:T(8,128)S(1)} %get-tuple-element.29), channel_id=1, source_target_pairs={{8,16},{16,8},{24,32},{32,24},{40,48},{48,40},{56,0},{0,56},{9,17}... | collective-permute-start | bytes 344072 | tf_op jit(solution)/shard_map/ppermute | solution.py:22
  17.5 1.9 %collective-permute-start.2 = (f32[7,16,256]{2,1,0:T(8,128)S(1)}, f32[7,16,256]{2,1,0:T(8,128)S(1)}, u32[]{:S(2)}, u32[]{:S(2)}) collective-permute-start(f32[7,16,256]{2,1,0:T(8,128)S(1)} %get-tuple-element.30), channel_id=1, source_target_pairs={{0,8},{8,0},{16,24},{24,16},{32,40},{40,32},{48,56},{56,48},{1,9},... | collective-permute-start | bytes 344072 | tf_op jit(solution)/shard_map/ppermute | solution.py:26
  19.4 0.0 collective-permute-done.ring
  19.4 0.0 copy-start.3
  19.4 0.8 %shard_map.69 = (f32[3,16,16,256]{3,2,1,0:T(8,128)S(1)}, f32[3,16,16,256]{3,2,1,0:T(8,128)S(1)}) custom-call(f32[3,16,16,256]{3,2,1,0:T(8,128)S(1)} %bitcast.12, f32[16,16,256]{2,1,0:T(8,128)S(1)} %bitcast.15, f32[3,16,16,256]{3,2,1,0:T(8,128)S(1)} %bitcast.21, f32[3,16,16,256]{3,2,1,0:T(8,128)S(1)} %copy-done.5, f32[18,16,256]{2,1,0:T(8,128)S(1)} %collective-permute-done.ring), custom_call_target="tpu_custom_call" | custom-call | flops 1000 | bytes 4489216 | tf_op jit(solution)/shard_map/pallas_call | solution.py:382
  20.2 0.8 %collective-permute-done.1.got_odd = f32[7,16,256]{2,1,0:T(8,128)S(1)} collective-permute-done((f32[7,16,256]{2,1,0:T(8,128)S(1)}, f32[7,16,256]{2,1,0:T(8,128)S(1)}, u32[]{:S(2)}, u32[]{:S(2)}) %collective-permute-start.1) | collective-permute-done | bytes 114720 | tf_op jit(solution)/shard_map/ppermute | solution.py:22
  21.0 0.0 collective-permute-done.2.got_even
  21.0 1.1 %shard_map.71 = (f32[7,16,256]{2,1,0:T(8,128)S(1)}, f32[7,16,256]{2,1,0:T(8,128)S(1)}, f32[16,16,256]{2,1,0:T(8,128)S(1)}, f32[12,16,256]{2,1,0:T(8,128)S(1)}, f...) custom-call(s32[2]{0:T(128)S(1)} %pad_add_fusion.parity, ...), custom_call_target="tpu_custom_call" | custom-call | flops 1000 | bytes 4767752 | tf_op jit(solution)/shard_map/pallas_call | solution.py:382
  22.1 5.7 %collective-permute-start.4 = (f32[12,16,256]{2,1,0:T(8,128)S(1)}, f32[12,16,256]{2,1,0:T(8,128)S(1)}, u32[]{:S(2)}, u32[]{:S(2)}) collective-permute-start(f32[12,16,256]{2,1,0:T(8,128)S(1)} %get-tuple-element.35), channel_id=1, source_target_pairs={{1,2},{2,1},{3,4},{4,3},{5,6},{6,5},{7,0},{0,7},{9,10},{10,9},{11,... | collective-permute-start | bytes 589832 | tf_op jit(solution)/shard_map/ppermute | solution.py:22
  27.9 1.9 %collective-permute-start.5 = (f32[12,16,256]{2,1,0:T(8,128)S(1)}, f32[12,16,256]{2,1,0:T(8,128)S(1)}, u32[]{:S(2)}, u32[]{:S(2)}) collective-permute-start(f32[12,16,256]{2,1,0:T(8,128)S(1)} %get-tuple-element.36), channel_id=1, source_target_pairs={{0,1},{1,0},{2,3},{3,2},{4,5},{5,4},{6,7},{7,6},{8,9},{9,8},{10,11... | collective-permute-start | bytes 589832 | tf_op jit(solution)/shard_map/ppermute | solution.py:26
  29.8 2.6 %collective-permute-start.3 = (f32[3,13,16,256]{3,2,1,0:T(8,128)S(1)}, f32[3,13,16,256]{3,2,1,0:T(8,128)S(1)}, u32[]{:S(2)}, u32[]{:S(2)}) collective-permute-start(f32[3,13,16,256]{3,2,1,0:T(8,128)S(1)} %get-tuple-element.31), channel_id=1, source_target_pairs={{0,64},{64,128},{128,192},{192,256},{256,320},{320,384},{384,448},... | collective-permute-start | bytes 1916936 | tf_op jit(solution)/shard_map/ppermute | solution.py:409
  32.4 1.1 %collective-permute-done.4.got_odd = f32[12,16,256]{2,1,0:T(8,128)S(1)} collective-permute-done((f32[12,16,256]{2,1,0:T(8,128)S(1)}, f32[12,16,256]{2,1,0:T(8,128)S(1)}, u32[]{:S(2)}, u32[]{:S(2)}) %collective-permute-start.4) | collective-permute-done | bytes 196640 | tf_op jit(solution)/shard_map/ppermute | solution.py:22
  33.5 2.6 %collective-permute-done.5.got_even = f32[12,16,256]{2,1,0:T(8,128)S(1)} collective-permute-done((f32[12,16,256]{2,1,0:T(8,128)S(1)}, f32[12,16,256]{2,1,0:T(8,128)S(1)}, u32[]{:S(2)}, u32[]{:S(2)}) %collective-permute-start.5) | collective-permute-done | bytes 196640 | tf_op jit(solution)/shard_map/ppermute | solution.py:26
  36.1 0.7 %shard_map.72 = (f32[12,16,256]{2,1,0:T(8,128)S(1)}, f32[12,16,256]{2,1,0:T(8,128)S(1)}, f32[8,16,256]{2,1,0:T(8,128)S(1)}, f32[3,24,256]{2,1,0:T(8,128)S(1)}, f32[3,24,256]{2,1,0:T(8,128)S(1)}) custom-call(s32[2]{0:T(128)S(1)} %pad_add_fusion.parity, f32[3,16,16,256]{3,2,1,0:T(8,128)S(1)} %get-tuple-element.27.flux0, ...), custom_call_target="tpu_custom_call" | custom-call | flops 20000000000 | bytes 3522568 | tf_op jit(solution)/shard_map/pallas_call | solution.py:382
  36.8 3.7 %collective-permute-start.6 = (f32[3,24,256]{2,1,0:T(8,128)S(1)}, f32[3,24,256]{2,1,0:T(8,128)S(1)}, u32[]{:S(2)}, u32[]{:S(2)}) collective-permute-start(f32[3,24,256]{2,1,0:T(8,128)S(1)} %get-tuple-element.48), channel_id=1, source_target_pairs={{8,16},{16,8},{24,32},{32,24},{40,48},{48,40},{56,0},{0,56},{9,17}... | collective-permute-start | bytes 221192 | tf_op jit(solution)/shard_map/ppermute | solution.py:22
  40.5 1.9 %collective-permute-start.7 = (f32[3,24,256]{2,1,0:T(8,128)S(1)}, f32[3,24,256]{2,1,0:T(8,128)S(1)}, u32[]{:S(2)}, u32[]{:S(2)}) collective-permute-start(f32[3,24,256]{2,1,0:T(8,128)S(1)} %get-tuple-element.49), channel_id=1, source_target_pairs={{0,8},{8,0},{16,24},{24,16},{32,40},{40,32},{48,56},{56,48},{1,9},... | collective-permute-start | bytes 221192 | tf_op jit(solution)/shard_map/ppermute | solution.py:26
  42.4 5.0 %collective-permute-done.3.prev = f32[3,13,16,256]{3,2,1,0:T(8,128)S(1)} collective-permute-done((f32[3,13,16,256]{3,2,1,0:T(8,128)S(1)}, f32[3,13,16,256]{3,2,1,0:T(8,128)S(1)}, u32[]{:S(2)}, u32[]{:S(2)}) %collective-permute-start.3) | collective-permute-done | bytes 639008 | tf_op jit(solution)/shard_map/ppermute | solution.py:409
  47.4 0.6 %shard_map.73 = (f32[3,16,16,256]{3,2,1,0:T(8,128)S(1)}, f32[16,24,256]{2,1,0:T(8,128)S(1)}, f32[16,24,256]{2,1,0:T(8,128)S(1)}, f32[1,24,256]{2,1,0:T(8,128)S(1...) custom-call(f32[3,16,16,256]{3,2,1,0:T(8,128)S(1)} %get-tuple-element.27.flux0, ...), custom_call_target="tpu_custom_call" | custom-call | flops 1000 | bytes 6266880 | tf_op jit(solution)/shard_map/pallas_call | solution.py:382
  48.0 2.3 %shard_map.74 = (f32[3,16,16,256]{3,2,1,0:T(8,128)}, f32[16,16,256]{2,1,0:T(8,128)}) custom-call(s32[2]{0:T(128)S(1)} %pad_add_fusion.parity, f32[3,16,16,256]{3,2,1,0:T(8,128)S(1)} %get-tuple-element.41.flux, f32[16,24,256]{2,1,0:T(8,128)S(1)} %get-tuple-element.42.own_c, f32[16,24,256]{2,1,0:T(8,128)S(1)} %get-tuple-element.43.own_scale, ...), custom_call_target="tpu_custom_call" | custom-call | flops 1000 | bytes 4464648 | tf_op jit(solution)/shard_map/pallas_call | solution.py:382
  (12 shorter events, 0.0 us)
Async XLA Ops:
  0.6 1.1 %copy-start = (f32[3,1,16,16,256]{4,3,2,1,0:T(8,128)S(1)}, f32[3,1,16,16,256]{4,3,2,1,0:T(8,128)}, u32[]{:S(2)}) copy-start(f32[3,1,16,16,256]{4,3,2,1,0:T(8,128)} %param.5) | copy-start | bytes 2359300
  1.8 5.0 %copy-start.1 = (f32[3,1,16,16,256]{4,3,2,1,0:T(8,128)S(1)}, f32[3,1,16,16,256]{4,3,2,1,0:T(8,128)}, u32[]{:S(2)}) copy-start(f32[3,1,16,16,256]{4,3,2,1,0:T(8,128)} %param.5) | copy-start | bytes 2359300
  1.8 5.0 %copy-start.2 = (f32[1,16,16,256]{3,2,1,0:T(8,128)S(1)}, f32[1,16,16,256]{3,2,1,0:T(8,128)}, u32[]{:S(2)}) copy-start(f32[1,16,16,256]{3,2,1,0:T(8,128)} %param.6) | copy-start | bytes 786436
  1.8 5.0 %copy-start.5 = (f32[3,16,16,256]{3,2,1,0:T(8,128)S(1)}, f32[3,16,16,256]{3,2,1,0:T(8,128)}, u32[]{:S(2)}) copy-start(f32[3,16,16,256]{3,2,1,0:T(8,128)} %visc.3) | copy-start | bytes 2359300
  1.9 17.6 %collective-permute-start = (f32[18,16,256]{2,1,0:T(8,128)S(1)}, f32[18,16,256]{2,1,0:T(8,128)S(1)}, u32[]{:S(2)}, u32[]{:S(2)}) collective-permute-start(f32[18,16,256]{2,1,0:T(8,128)S(1)} %shard_map.68), channel_id=1, source_target_pairs={{0,64},{64,128},{128,192},{192,256},{256,320},{320,384},{384,448},... | collective-permute-start | bytes 884744 | tf_op jit(solution)/shard_map/ppermute | solution.py:402
  6.8 12.6 %copy-start.4 = (f32[3,1,16,16,256]{4,3,2,1,0:T(8,128)S(1)}, f32[3,1,16,16,256]{4,3,2,1,0:T(8,128)}, u32[]{:S(2)}) copy-start(f32[3,1,16,16,256]{4,3,2,1,0:T(8,128)} %param.7) | copy-start | bytes 2359300
  7.4 13.7 %collective-permute-start.1 = (f32[7,16,256]{2,1,0:T(8,128)S(1)}, f32[7,16,256]{2,1,0:T(8,128)S(1)}, u32[]{:S(2)}, u32[]{:S(2)}) collective-permute-start(f32[7,16,256]{2,1,0:T(8,128)S(1)} %get-tuple-element.29), channel_id=1, source_target_pairs={{8,16},{16,8},{24,32},{32,24},{40,48},{48,40},{56,0},{0,56},{9,17}... | collective-permute-start | bytes 344072 | tf_op jit(solution)/shard_map/ppermute | solution.py:22
  17.5 3.6 %collective-permute-start.2 = (f32[7,16,256]{2,1,0:T(8,128)S(1)}, f32[7,16,256]{2,1,0:T(8,128)S(1)}, u32[]{:S(2)}, u32[]{:S(2)}) collective-permute-start(f32[7,16,256]{2,1,0:T(8,128)S(1)} %get-tuple-element.30), channel_id=1, source_target_pairs={{0,8},{8,0},{16,24},{24,16},{32,40},{40,32},{48,56},{56,48},{1,9},... | collective-permute-start | bytes 344072 | tf_op jit(solution)/shard_map/ppermute | solution.py:26
  19.4 1.6 %copy-start.3 = (f32[1,16,16,256]{3,2,1,0:T(8,128)S(1)}, f32[1,16,16,256]{3,2,1,0:T(8,128)}, u32[]{:S(2)}) copy-start(f32[1,16,16,256]{3,2,1,0:T(8,128)} %param.8) | copy-start | bytes 786436
  22.1 11.3 %collective-permute-start.4 = (f32[12,16,256]{2,1,0:T(8,128)S(1)}, f32[12,16,256]{2,1,0:T(8,128)S(1)}, u32[]{:S(2)}, u32[]{:S(2)}) collective-permute-start(f32[12,16,256]{2,1,0:T(8,128)S(1)} %get-tuple-element.35), channel_id=1, source_target_pairs={{1,2},{2,1},{3,4},{4,3},{5,6},{6,5},{7,0},{0,7},{9,10},{10,9},{11,... | collective-permute-start | bytes 589832 | tf_op jit(solution)/shard_map/ppermute | solution.py:22
  27.9 8.2 %collective-permute-start.5 = (f32[12,16,256]{2,1,0:T(8,128)S(1)}, f32[12,16,256]{2,1,0:T(8,128)S(1)}, u32[]{:S(2)}, u32[]{:S(2)}) collective-permute-start(f32[12,16,256]{2,1,0:T(8,128)S(1)} %get-tuple-element.36), channel_id=1, source_target_pairs={{0,1},{1,0},{2,3},{3,2},{4,5},{5,4},{6,7},{7,6},{8,9},{9,8},{10,11... | collective-permute-start | bytes 589832 | tf_op jit(solution)/shard_map/ppermute | solution.py:26
  29.8 17.6 %collective-permute-start.3 = (f32[3,13,16,256]{3,2,1,0:T(8,128)S(1)}, f32[3,13,16,256]{3,2,1,0:T(8,128)S(1)}, u32[]{:S(2)}, u32[]{:S(2)}) collective-permute-start(f32[3,13,16,256]{3,2,1,0:T(8,128)S(1)} %get-tuple-element.31), channel_id=1, source_target_pairs={{0,64},{64,128},{128,192},{192,256},{256,320},{320,384},{384,448},... | collective-permute-start | bytes 1916936 | tf_op jit(solution)/shard_map/ppermute | solution.py:409
  36.8 11.2 %collective-permute-start.6 = (f32[3,24,256]{2,1,0:T(8,128)S(1)}, f32[3,24,256]{2,1,0:T(8,128)S(1)}, u32[]{:S(2)}, u32[]{:S(2)}) collective-permute-start(f32[3,24,256]{2,1,0:T(8,128)S(1)} %get-tuple-element.48), channel_id=1, source_target_pairs={{8,16},{16,8},{24,32},{32,24},{40,48},{48,40},{56,0},{0,56},{9,17}... | collective-permute-start | bytes 221192 | tf_op jit(solution)/shard_map/ppermute | solution.py:22
  40.5 7.5 %collective-permute-start.7 = (f32[3,24,256]{2,1,0:T(8,128)S(1)}, f32[3,24,256]{2,1,0:T(8,128)S(1)}, u32[]{:S(2)}, u32[]{:S(2)}) collective-permute-start(f32[3,24,256]{2,1,0:T(8,128)S(1)} %get-tuple-element.49), channel_id=1, source_target_pairs={{0,8},{8,0},{16,24},{24,16},{32,40},{40,32},{48,56},{56,48},{1,9},... | collective-permute-start | bytes 221192 | tf_op jit(solution)/shard_map/ppermute | solution.py:26

commit v3 on v2

--- a/solution.py
+++ b/solution.py
@@ -62,6 +62,21 @@
                     tile, row = divmod(len(single), ny)
                     single[c, i, j] = (len(whole) + tile, row)
     return whole, single, lines, len(whole) + -(-len(single) // ny)
+
+
+def bulk_plan(nx, ny):
+    whole = ring_plan(nx, ny)[0]
+    start, used = {}, 2
+    for c in range(3):
+        for i in range(nx):
+            if (c, i) not in whole:
+                start[c, i] = used
+                used += inner_rows(c, ny)
+    return start, -(-(used + 4) // 8) * 8
+
+
+def inner_rows(c, ny):
+    return ny - (4 if c == 1 else 3)
 
 
 def share(c):
@@ -128,7 +143,7 @@
             flux[c, i] = k * (f[c, i] + prev + nu * near - slope) + flow * (1.0 - 1.0 / RELAX)
 
 
-def edge_kernel(parity, flux0, coeff, v, p, s, got_odd, got_even, lo_x, hi_x, total, send_odd, send_even, own, inner):
+def edge_kernel(parity, flux0, coeff, v, p, s, got_odd, got_even, lo_x, hi_x, total, send_odd, send_even, own):
     nx, ny = s.shape[0], s.shape[1]
     shape = s.shape[1:]
     rows = row_id(shape)
@@ -140,16 +155,15 @@
         lo_x[layer], hi_x[layer] = pick(parity[0] == 0, got_odd, got_even, layer)
 
     def send(layer, i, up, down):
-        send_even[layer, i : i + 1, :] = jnp.where(even_y, up, down)
-        send_odd[layer, i : i + 1, :] = jnp.where(even_y, down, up)
+        row = layer * nx + i
+        send_even[row : row + 1, :] = jnp.where(even_y, up, down)
+        send_odd[row : row + 1, :] = jnp.where(even_y, down, up)
 
     before = None
     for i in range(nx):
         row = slice(i, i + 1)
         flows = []
         for c in range(3):
-            if 1 < i < nx - 1:
-                inner[c, i - 2] = v[c, i]
             k = coeff[c, i]
             value = flux0[c, i]
             if i == 0:
@@ -181,12 +195,12 @@
         send(3, i, flows[1][top], p[i, low, :])
         send(7, i, right[top], right[low])
         send(8, i, over[top], right[near])
-        send(9, i, zero, tot[low])
-        send(10, i, zero, over[near])
-    send(11, 0, before[top], before[low])
-    send(11, 1, zero, before[near])
-    for i in range(2, nx):
-        send(11, i, zero, zero)
+        send(9, i, zero, over[near])
+    send(10, 0, before[top], before[low])
+    send(10, 1, zero, before[near])
+    send(10, 2, zero, lo_x[4, low, :])
+    for i in range(3, 8):
+        send(10, i, zero, zero)
 
 
 def extend(dst, index, own, r16, r17, low):
@@ -195,6 +209,16 @@
     dst[index, n : n + 1, :] = r16
     dst[index, n + 1 : n + 2, :] = r17
     dst[index, EXT - 1 : EXT, :] = low
+
+
+def bulk_kernel(v, _, bulk):
+    ny = v.shape[2]
+    start, size = bulk_plan(v.shape[1], ny)
+    bulk[0:8, :] = jnp.zeros((8, bulk.shape[1]), jnp.float32)
+    bulk[size - 8 :, :] = jnp.zeros((8, bulk.shape[1]), jnp.float32)
+    for (c, i), row in start.items():
+        count = inner_rows(c, ny)
+        bulk[row : row + count, :] = v[c, i, 2 : 2 + count, :]
 
 
 def whole_flux(c, i, flux0, coeff, prev, lo_x, hi_x, lo_y, hi_y, rows):
@@ -208,10 +232,10 @@
     if i == nx - 1:
         near = near + hi_x[c]
     value = flux0[c, i] + share(k) * near
-    whole, _, lines, _ = ring_plan(nx, ny)
-    if (c, i) not in whole:
+    if (c, i) not in ring_plan(nx, ny)[0]:
         inside = (rows > 1) & (rows < ny - (2 if c == 1 else 1))
-        value = value + k * jnp.where(inside, prev[c, i - 2], 0.0)
+        begin = bulk_plan(nx, ny)[0][c, i] - 2
+        value = value + k * jnp.where(inside, prev[begin : begin + ny, :], 0.0)
     if c == 0 and i == nx - 1:
         value = value - k * hi_x[3]
     if c == 1:
@@ -242,8 +266,9 @@
     even_x, even_y = parity[0] == 0, parity[1] == 0
     rows = row_id(s.shape[1:])
     first = rows == 0
-    for layer in range(12):
-        lo_y[layer], hi_y[layer] = pick(even_y, got_odd, got_even, layer)
+    for layer in range(10):
+        lo_y[layer], hi_y[layer] = pick(even_y, got_odd, got_even, slice(layer * nx, layer * nx + nx))
+    lo_few, hi_few = pick(even_y, got_odd, got_even, slice(10 * nx, 10 * nx + 8))
 
     def along_x(x):
         return x - jnp.where(first_x, 0.0, pltpu.roll(x, 1, 0))
@@ -255,15 +280,16 @@
     out_rows[0] = lo_y[3] + push_y
     out_rows[1] = lo_y[7] + along_x(edge) + push_y + push_z - below_z(push_z)
     out_rows[5] = lo_y[8]
-    side_low = lo_y[11, 0:1, :] + edge[nx - 1 :]
+    side_low = lo_few[0:1] + edge[nx - 1 :]
     edge = share(hi_y[4]) * own[3]
     push_y = share(hi_y[5]) * own[4]
     push_z = share(hi_y[6]) * own[5]
     out_rows[2] = hi_y[7] + along_x(edge) + push_y + push_z - below_z(push_z)
     out_rows[3] = hi_y[8] - push_y
-    out_rows[4] = -DAMPING / (hi_y[9] + own[7])
-    out_rows[6] = hi_y[10]
-    side_16, side_17 = hi_y[11, 0:1, :] + edge[nx - 1 :], hi_y[11, 1:2, :]
+    before = jnp.where(first_x, hi_few[2:3], pltpu.roll(hi_y[4], 1, 0))
+    out_rows[4] = -DAMPING / (hi_y[4] + before + hi_y[5] + own[7] + hi_y[6] + below_z(hi_y[6]))
+    out_rows[6] = hi_y[9]
+    side_16, side_17 = hi_few[0:1] + edge[nx - 1 :], hi_few[1:2]
 
     right_x[...] = jnp.zeros_like(right_x)
     scale_x[...] = jnp.zeros_like(scale_x)
@@ -293,9 +319,17 @@
     send(2, jnp.zeros(side.shape[1:], jnp.float32), scale_x[0])
 
 
+def sweep(low, mid, high, below_kx, kx, ky, kz, scale):
+    gx = kx * (high - mid) - below_kx * (mid - low)
+    gy = ky * (above_y(mid) - mid)
+    gz = kz * (above_z(mid) - mid)
+    applied = gx + gy - below_y(gy) + gz - below_z(gz)
+    return 2.0 * mid - scale * applied
+
+
 def own_kernel(
-    flux0, coeff, prev, s, total, lo_x, hi_x, lo_y, hi_y, out_rows,
-    flux, first_c, scale_x, side, kx, ky, kz,
+    flux0, coeff, prev, s, p, total, lo_x, hi_x, lo_y, hi_y, out_rows,
+    flux, first_c, scale_x, side, kx, ky, kz, ends, wide_v, wide_p,
 ):
     nx, ny = s.shape[0], s.shape[1]
     rows = row_id(s.shape[1:])
@@ -317,13 +351,33 @@
         extend(ky, i, coeff[1, i], hi_y[5, row, :], zero, lo_y[5, row, :])
         extend(kz, i, coeff[2, i], hi_y[6, row, :], zero, zero)
     extend(side, 0, before, out_rows[7, 1:2, :], out_rows[7, 2:3, :], out_rows[7, 0:1, :])
+    now = None
+    for i in range(2, nx - 1):
+        after = sweep(first_c[i - 1], first_c[i], first_c[i + 1], kx[i - 1], kx[i], ky[i], kz[i], scale_x[i])
+        wide_p[i - 2] = p[i] + after[:ny]
+        wide_v[1, i - 2] = flux[1, i] - coeff[1, i] * (above_y(after) - after)[:ny]
+        wide_v[2, i - 2] = flux[2, i] - coeff[2, i] * (above_z(after) - after)[:ny]
+        if now is None:
+            ends[0] = after
+        else:
+            wide_v[0, i - 3] = flux[0, i - 1] - coeff[0, i - 1] * (after - now)[:ny]
+        now = after
+    ends[1] = now
 
 
 def last_kernel(
-    parity, flux, own_c, own_scale, side, own_kx, own_ky, own_kz, p, lo_x, hi_x, got_odd, got_even,
-    new_v, new_p, edge,
+    parity, flux, own_c, own_scale, side, own_kx, own_ky, own_kz, ends, p, lo_x, hi_x, got_odd, got_even, wide_v, wide_p,
+    new_v, new_p, edge, low_v, low_p, top_v, top_p, top_x, sems,
 ):
     nx, ny = p.shape[0], p.shape[1]
+    ready = [
+        pltpu.make_async_copy(wide_v.at[0, pl.ds(0, nx - 4)], new_v.at[0, pl.ds(2, nx - 4)], sems.at[5]),
+        pltpu.make_async_copy(wide_v.at[1], new_v.at[1, pl.ds(2, nx - 3)], sems.at[6]),
+        pltpu.make_async_copy(wide_v.at[2], new_v.at[2, pl.ds(2, nx - 3)], sems.at[7]),
+        pltpu.make_async_copy(wide_p, new_p.at[pl.ds(2, nx - 3)], sems.at[8]),
+    ]
+    for copy in ready:
+        copy.start()
     even_x = parity[0] == 0
     lo0, hi0 = pick(even_x, got_odd, got_even, 0)
     lo1, hi1 = pick(even_x, got_odd, got_even, 1)
@@ -335,56 +389,62 @@
     edge[2, 0:ny, :] = hi_x[5]
     edge[2, EXT - 1 : EXT, :] = hi2[ny + 2 : ny + 3, :]
     edge[3, 0:ny, :] = hi_x[6]
-
-    def first_c(i):
-        if i == -1:
-            return lo0
-        if i == 0:
-            return own_c[0] - lo1 * own_scale[0]
-        if i == nx:
-            return (hi1 - side[0]) * hi2
-        if i == nx + 1:
-            return hi0
-        return own_c[i]
-
-    def sweep(i, low, mid, high):
-        if i < nx:
-            kx, ky, kz, scale = own_kx[i], own_ky[i], own_kz[i], own_scale[i]
-        else:
-            kx, ky, kz, scale = edge[1], edge[2], edge[3], hi2
-        below_kx = own_kx[i - 1] if i > 0 else edge[0]
-        gx = kx * (high - mid) - below_kx * (mid - low)
-        gy = ky * (above_y(mid) - mid)
-        gz = kz * (above_z(mid) - mid)
-        applied = gx + gy - below_y(gy) + gz - below_z(gz)
-        return 2.0 * mid - scale * applied
-
-    low, mid, high = first_c(-1), first_c(0), first_c(1)
-    now = sweep(0, low, mid, high)
-    for i in range(nx):
-        low, mid, high = mid, high, first_c(i + 2)
-        after = sweep(i + 1, low, mid, high)
-        new_p[i] = p[i] + now[:ny]
-        new_v[0, i] = flux[0, i] - own_kx[i, :ny] * (after - now)[:ny]
-        new_v[1, i] = flux[1, i] - own_ky[i, :ny] * (above_y(now) - now)[:ny]
-        new_v[2, i] = flux[2, i] - own_kz[i, :ny] * (above_z(now) - now)[:ny]
-        now = after
+    zeroth = own_c[0] - lo1 * own_scale[0]
+    beyond = (hi1 - side[0]) * hi2
+    at = lambda i: (own_kx[i], own_ky[i], own_kz[i], own_scale[i])
+    second = {
+        0: sweep(lo0, zeroth, own_c[1], edge[0], *at(0)),
+        1: sweep(zeroth, own_c[1], own_c[2], own_kx[0], *at(1)),
+        2: ends[0],
+        nx - 2: ends[1],
+        nx - 1: sweep(own_c[nx - 2], own_c[nx - 1], beyond, own_kx[nx - 2], *at(nx - 1)),
+        nx: sweep(own_c[nx - 1], beyond, hi0, own_kx[nx - 1], edge[1], edge[2], edge[3], hi2),
+    }
+
+    def step_x(i):
+        return flux[0, i] - own_kx[i, :ny] * (second[i + 1] - second[i])[:ny]
+
+    def step_y(i):
+        return flux[1, i] - own_ky[i, :ny] * (above_y(second[i]) - second[i])[:ny]
+
+    def step_z(i):
+        return flux[2, i] - own_kz[i, :ny] * (above_z(second[i]) - second[i])[:ny]
+
+    for n, i in enumerate((0, 1)):
+        low_v[0, n], low_v[1, n], low_v[2, n] = step_x(i), step_y(i), step_z(i)
+        low_p[n] = p[i] + second[i][:ny]
+    top_v[0, 0], top_v[1, 0], top_v[2, 0] = step_x(nx - 1), step_y(nx - 1), step_z(nx - 1)
+    top_p[0] = p[nx - 1] + second[nx - 1][:ny]
+    top_x[0] = step_x(nx - 2)
+    copies = [
+        pltpu.make_async_copy(low_v, new_v.at[:, pl.ds(0, 2)], sems.at[0]),
+        pltpu.make_async_copy(top_v, new_v.at[:, pl.ds(nx - 1, 1)], sems.at[1]),
+        pltpu.make_async_copy(top_x, new_v.at[0, pl.ds(nx - 2, 1)], sems.at[2]),
+        pltpu.make_async_copy(low_p, new_p.at[pl.ds(0, 2)], sems.at[3]),
+        pltpu.make_async_copy(top_p, new_p.at[pl.ds(nx - 1, 1)], sems.at[4]),
+    ]
+    for copy in copies:
+        copy.start()
+    for copy in ready + copies:
+        copy.wait()
 
 
 VM = pl.BlockSpec(memory_space=pltpu.VMEM)
 SM = pl.BlockSpec(memory_space=pltpu.SMEM)
 
 
-def call(kernel, args, outs, scratch=(), scalars=True, flops=1000):
+ANY = pl.BlockSpec(memory_space=pl.ANY)
+
+
+def call(kernel, args, outs, scratch=(), scalars=True, flops=1000, far=0):
     shapes = [jax.ShapeDtypeStruct(s, jnp.float32) for s in outs]
     size = sum(4 * a.size for a in args) + sum(4 * s.size for s in shapes)
-    specs = [SM] + [VM] * (len(args) - 1) if scalars else [VM] * len(args)
     return pl.pallas_call(
         kernel,
         out_shape=shapes,
-        in_specs=specs,
-        out_specs=[VM] * len(shapes),
-        scratch_shapes=[pltpu.VMEM(s, jnp.float32) for s in scratch],
+        in_specs=[SM] * scalars + [VM] * (len(args) - scalars),
+        out_specs=[VM] * (len(shapes) - far) + [ANY] * far,
+        scratch_shapes=[pltpu.VMEM(s, jnp.float32) for s in scratch] + [pltpu.SemaphoreType.DMA((9,))] * (far > 0),
         compiler_params=pltpu.CompilerParams(vmem_limit_bytes=40 * 2**20),
         cost_estimate=pl.CostEstimate(flops=flops, bytes_accessed=size, transcendentals=0),
     )(*args)
@@ -401,32 +461,36 @@
     odd_x, even_x = swap_odd(face_odd, "gx"), swap_even(face_even, "gx")
     ring = lax.ppermute(ring, "ta", ahead)
     flux0, coeff = call(local_kernel, (v, p, f, viscosity, ring), (v.shape,) * 2, scalars=False)
-    lo_x, hi_x, total, send_odd, send_even, own, inner = call(
+    lo_x, hi_x, total, send_odd, send_even, own = call(
         edge_kernel,
         (parity, flux0, coeff, v, p, s, odd_x, even_x),
-        ((7, ny, nz), (7, ny, nz), p.shape, (12, nx, nz), (12, nx, nz), (8, nx, nz), (3, nx - 3, ny, nz)),
-    )
-    prev = lax.ppermute(inner, "ta", ahead)
+        ((7, ny, nz), (7, ny, nz), p.shape, (10 * nx + 8, nz), (10 * nx + 8, nz), (8, nx, nz)),
+    )
+    (bulk,) = call(bulk_kernel, (v, total), ((bulk_plan(nx, ny)[1], nz),), scalars=False)
+    prev = lax.ppermute(bulk, "ta", ahead)
     odd_y, even_y = swap_odd(send_odd, "gy"), swap_even(send_even, "gy")
     lo_y, hi_y, out_rows, send_odd, send_even = call(
         strip_kernel,
         (parity, flux0, coeff, s, total, lo_x, hi_x, odd_y, even_y, own),
-        ((12, nx, nz), (12, nx, nz), (8, nx, nz), (3, EXT, nz), (3, EXT, nz)),
+        ((10, nx, nz), (10, nx, nz), (8, nx, nz), (3, EXT, nz), (3, EXT, nz)),
         ((3, EXT, nz), (3, EXT, nz), (1, EXT, nz)),
         flops=20_000_000_000,
     )
     odd_x, even_x = swap_odd(send_odd, "gx"), swap_even(send_even, "gx")
-    flux, first_c, scale, side, kx, ky, kz = call(
+    flux, first_c, scale, side, kx, ky, kz, ends, wide_v, wide_p = call(
         own_kernel,
-        (flux0, coeff, prev, s, total, lo_x, hi_x, lo_y, hi_y, out_rows),
-        (v.shape, (nx, EXT, nz), (nx, EXT, nz), (1, EXT, nz)) + ((nx, EXT, nz),) * 3,
+        (flux0, coeff, prev, s, p, total, lo_x, hi_x, lo_y, hi_y, out_rows),
+        (v.shape, (nx, EXT, nz), (nx, EXT, nz), (1, EXT, nz))
+        + ((nx, EXT, nz),) * 3
+        + ((2, EXT, nz), (3, nx - 3, ny, nz), (nx - 3, ny, nz)),
         scalars=False,
     )
     new_v, new_p = call(
         last_kernel,
-        (parity, flux, first_c, scale, side, kx, ky, kz, p, lo_x, hi_x, odd_x, even_x),
+        (parity, flux, first_c, scale, side, kx, ky, kz, ends, p, lo_x, hi_x, odd_x, even_x, wide_v, wide_p),
         (v.shape, p.shape),
-        ((4, EXT, nz),),
+        ((4, EXT, nz), (3, 2, ny, nz), (2, ny, nz), (3, 1, ny, nz), (1, ny, nz), (1, ny, nz)),
+        far=2,
     )
     return new_v[:, None], new_p[None]
 

time: 50.6 us -> 47.7 us (0.943)
  waiting for transfers between devices: 9.51 us -> 6.6 us
    ppermute x1, waiting for transfers between devices: 5.01 us -> 2.8 us  [body(): prev = lax.ppermute(bulk, 'ta', ahead)]
    ppermute x3, waiting for transfers between devices: 1.89 us -> 0.96 us  [swap_odd(): return lax.ppermute(x, axis, odd_pairs(lax.axis_size(axis)))]
    pallas_call x7 -> x8, Pallas kernels: 6.09 us -> 6.16 us  [call(): pl.pallas_call(kernel, out_shape=shapes, in_specs=[SM] * scalars + [VM] *...]
  transfers between devices with their start and end apart: 8 -> 8, of which waited for: 4 -> 4; matrix products, arithmetic and copies ran while one was open for 0% -> 0% of each run, Pallas kernels for 5% -> 7%
where the time goes in v3:
time: 47.7 us; the launch traced here: 47.4 us
  starting transfers between devices  32.6 us (68%)
  waiting for transfers between devices  6.6 us (14%)
  Pallas kernels  6.16 us (13%)
  local copies, waits for them, and re-layouts  1.15 us (2%)
  between operations  0.81 us (2%)
    ppermute x3, starting transfers between devices, swap_odd(): return lax.ppermute(x, axis, odd_pairs(lax.axis_size(axis)))  19.2 us
    pallas_call x8, Pallas kernels, call(): pl.pallas_call(kernel, out_shape=shapes, in_specs=[SM] * scalars + [VM] *...  6.16 us
    ppermute x3, starting transfers between devices, swap_even(): return lax.ppermute(x, axis, even_pairs(lax.axis_size(axis)))  5.99 us
    ppermute x1, starting transfers between devices, body(): ring = lax.ppermute(ring, 'ta', ahead)  4.83 us
    ppermute x3, waiting for transfers between devices, swap_even(): return lax.ppermute(x, axis, even_pairs(lax.axis_size(axis)))  2.83 us
    ppermute x1, waiting for transfers between devices, body(): prev = lax.ppermute(bulk, 'ta', ahead)  2.8 us
    ppermute x1, starting transfers between devices, body(): prev = lax.ppermute(bulk, 'ta', ahead)  2.59 us
    unnamed x12, local copies, waits for them, and re-layouts  1.15 us
  transfers between devices with their start and end apart: 8, of which 4 were waited for; matrix products, arithmetic and copies ran while one was open for 0% of the time, Pallas kernels for 7%

profile of v3, /device:TPU:24, one launch (start us, length us, event | category | flops | bytes accessed | tf_op | source)
XLA Modules:
  0.0 47.4 jit_solution(279720699552432817)
XLA Ops:
  0.6 1.1 %copy-done = f32[3,1,16,16,256]{4,3,2,1,0:T(8,128)S(1)} copy-done((f32[3,1,16,16,256]{4,3,2,1,0:T(8,128)S(1)}, f32[3,1,16,16,256]{4,3,2,1,0:T(8,128)}, u32[]{:S(2)}) %copy-start) | copy-done | bytes 786456
  1.8 0.1 shard_map.68
  1.9 4.8 %collective-permute-start = (f32[18,16,256]{2,1,0:T(8,128)S(1)}, f32[18,16,256]{2,1,0:T(8,128)S(1)}, u32[]{:S(2)}, u32[]{:S(2)}) collective-permute-start(f32[18,16,256]{2,1,0:T(8,128)S(1)} %shard_map.68), channel_id=1, source_target_pairs={{0,64},{64,128},{128,192},{192,256},{256,320},{320,384},{384,448},... | collective-permute-start | bytes 884744 | tf_op jit(solution)/shard_map/ppermute | solution.py:462
  6.7 0.1 pad_add_fusion.parity
  6.8 0.6 %shard_map.70 = (f32[7,16,256]{2,1,0:T(8,128)S(1)}, f32[7,16,256]{2,1,0:T(8,128)S(1)}) custom-call(s32[2]{0:T(128)S(1)} %pad_add_fusion.parity, f32[3,16,16,256]{3,2,1,0:T(8,128)S(1)} %bitcast.11, f32[16,16,256]{2,1,0:T(8,128)S(1)} %bitcast.15, f32[3,16,16,256]{3,2,1,0:T(8,128)S(1)} %copy-done.5), custom_call_target="tpu_custom_call" | custom-call | flops 20000000000 | bytes 2064392 | tf_op jit(solution)/shard_map/pallas_call | solution.py:442
  7.4 10.1 %collective-permute-start.1 = (f32[7,16,256]{2,1,0:T(8,128)S(1)}, f32[7,16,256]{2,1,0:T(8,128)S(1)}, u32[]{:S(2)}, u32[]{:S(2)}) collective-permute-start(f32[7,16,256]{2,1,0:T(8,128)S(1)} %get-tuple-element.31), channel_id=1, source_target_pairs={{8,16},{16,8},{24,32},{32,24},{40,48},{48,40},{56,0},{0,56},{9,17}... | collective-permute-start | bytes 344072 | tf_op jit(solution)/shard_map/ppermute | solution.py:22
  17.5 1.9 %collective-permute-start.2 = (f32[7,16,256]{2,1,0:T(8,128)S(1)}, f32[7,16,256]{2,1,0:T(8,128)S(1)}, u32[]{:S(2)}, u32[]{:S(2)}) collective-permute-start(f32[7,16,256]{2,1,0:T(8,128)S(1)} %get-tuple-element.32), channel_id=1, source_target_pairs={{0,8},{8,0},{16,24},{24,16},{32,40},{40,32},{48,56},{56,48},{1,9},... | collective-permute-start | bytes 344072 | tf_op jit(solution)/shard_map/ppermute | solution.py:26
  19.4 0.0 collective-permute-done.ring
  19.4 0.0 copy-start.3
  19.4 0.8 %shard_map.69 = (f32[3,16,16,256]{3,2,1,0:T(8,128)S(1)}, f32[3,16,16,256]{3,2,1,0:T(8,128)S(1)}) custom-call(f32[3,16,16,256]{3,2,1,0:T(8,128)S(1)} %bitcast.12, f32[16,16,256]{2,1,0:T(8,128)S(1)} %bitcast.16, f32[3,16,16,256]{3,2,1,0:T(8,128)S(1)} %bitcast.23, f32[3,16,16,256]{3,2,1,0:T(8,128)S(1)} %copy-done.5, f32[18,16,256]{2,1,0:T(8,128)S(1)} %collective-permute-done.ring), custom_call_target="tpu_custom_call" | custom-call | flops 1000 | bytes 4489216 | tf_op jit(solution)/shard_map/pallas_call | solution.py:442
  20.2 0.8 %collective-permute-done.1.got_odd = f32[7,16,256]{2,1,0:T(8,128)S(1)} collective-permute-done((f32[7,16,256]{2,1,0:T(8,128)S(1)}, f32[7,16,256]{2,1,0:T(8,128)S(1)}, u32[]{:S(2)}, u32[]{:S(2)}) %collective-permute-start.1) | collective-permute-done | bytes 114720 | tf_op jit(solution)/shard_map/ppermute | solution.py:22
  21.0 1.0 %shard_map.71 = (f32[7,16,256]{2,1,0:T(8,128)S(1)}, f32[7,16,256]{2,1,0:T(8,128)S(1)}, f32[16,16,256]{2,1,0:T(8,128)S(1)}, f32[168,256]{1,0:T(8,128)S(1)}, f32[1...) custom-call(s32[2]{0:T(128)S(1)} %pad_add_fusion.parity, f32[3,16,16,256]{3,2,1,0:T(8,128)S(1)} %get-tuple-element.29.flux0, ...), custom_call_target="tpu_custom_call" | custom-call | flops 1000 | bytes 4079624 | tf_op jit(solution)/shard_map/pallas_call | solution.py:442
  22.1 5.7 %collective-permute-start.4 = (f32[168,256]{1,0:T(8,128)S(1)}, f32[168,256]{1,0:T(8,128)S(1)}, u32[]{:S(2)}, u32[]{:S(2)}) collective-permute-start(f32[168,256]{1,0:T(8,128)S(1)} %get-tuple-element.36), channel_id=1, source_target_pairs={{1,2},{2,1},{3,4},{4,3},{5,6},{6,5},{7,0},{0,7},{9,10},{10,9},{11,... | collective-permute-start | bytes 516104 | tf_op jit(solution)/shard_map/ppermute | solution.py:22
  27.8 1.9 %collective-permute-start.5 = (f32[168,256]{1,0:T(8,128)S(1)}, f32[168,256]{1,0:T(8,128)S(1)}, u32[]{:S(2)}, u32[]{:S(2)}) collective-permute-start(f32[168,256]{1,0:T(8,128)S(1)} %get-tuple-element.37), channel_id=1, source_target_pairs={{0,1},{1,0},{2,3},{3,2},{4,5},{5,4},{6,7},{7,6},{8,9},{9,8},{10,11... | collective-permute-start | bytes 516104 | tf_op jit(solution)/shard_map/ppermute | solution.py:26
  29.7 0.1 shard_map.72
  29.8 2.6 %collective-permute-start.3 = (f32[488,256]{1,0:T(8,128)S(1)}, f32[488,256]{1,0:T(8,128)S(1)}, u32[]{:S(2)}, u32[]{:S(2)}) collective-permute-start(f32[488,256]{1,0:T(8,128)S(1)} %shard_map.72), channel_id=1, source_target_pairs={{0,64},{64,128},{128,192},{192,256},{256,320},{320,384},{384,448},... | collective-permute-start | bytes 1499144 | tf_op jit(solution)/shard_map/ppermute | solution.py:470
  32.4 0.2 collective-permute-done.4.got_odd
  32.6 2.8 %collective-permute-done.5.got_even = f32[168,256]{1,0:T(8,128)S(1)} collective-permute-done((f32[168,256]{1,0:T(8,128)S(1)}, f32[168,256]{1,0:T(8,128)S(1)}, u32[]{:S(2)}, u32[]{:S(2)}) %collective-permute-start.5) | collective-permute-done | bytes 172064 | tf_op jit(solution)/shard_map/ppermute | solution.py:26
  35.4 0.7 %shard_map.73 = (f32[10,16,256]{2,1,0:T(8,128)S(1)}, f32[10,16,256]{2,1,0:T(8,128)S(1)}, f32[8,16,256]{2,1,0:T(8,128)S(1)}, f32[3,24,256]{2,1,0:T(8,128)S(1)}, f32[3,24,256]{2,1,0:T(8,128)S(1)}) custom-call(s32[2]{0:T(128)S(1)} %pad_add_fusion.parity, f32[3,16,16,256]{3,2,1,0:T(8,128)S(1)} %get-tuple-element.29.flux0, ...), custom_call_target="tpu_custom_call" | custom-call | flops 20000000000 | bytes 3407880 | tf_op jit(solution)/shard_map/pallas_call | solution.py:442
  36.1 3.4 %collective-permute-start.6 = (f32[3,24,256]{2,1,0:T(8,128)S(1)}, f32[3,24,256]{2,1,0:T(8,128)S(1)}, u32[]{:S(2)}, u32[]{:S(2)}) collective-permute-start(f32[3,24,256]{2,1,0:T(8,128)S(1)} %get-tuple-element.50), channel_id=1, source_target_pairs={{8,16},{16,8},{24,32},{32,24},{40,48},{48,40},{56,0},{0,56},{9,17}... | collective-permute-start | bytes 221192 | tf_op jit(solution)/shard_map/ppermute | solution.py:22
  39.5 2.1 %collective-permute-start.7 = (f32[3,24,256]{2,1,0:T(8,128)S(1)}, f32[3,24,256]{2,1,0:T(8,128)S(1)}, u32[]{:S(2)}, u32[]{:S(2)}) collective-permute-start(f32[3,24,256]{2,1,0:T(8,128)S(1)} %get-tuple-element.51), channel_id=1, source_target_pairs={{0,8},{8,0},{16,24},{24,16},{32,40},{40,32},{48,56},{56,48},{1,9},... | collective-permute-start | bytes 221192 | tf_op jit(solution)/shard_map/ppermute | solution.py:26
  41.6 2.8 %collective-permute-done.3.prev = f32[488,256]{1,0:T(8,128)S(1)} collective-permute-done((f32[488,256]{1,0:T(8,128)S(1)}, f32[488,256]{1,0:T(8,128)S(1)}, u32[]{:S(2)}, u32[]{:S(2)}) %collective-permute-start.3) | collective-permute-done | bytes 499744 | tf_op jit(solution)/shard_map/ppermute | solution.py:470
  44.4 1.2 %shard_map.74 = (f32[3,16,16,256]{3,2,1,0:T(8,128)S(1)}, f32[16,24,256]{2,1,0:T(8,128)S(1)}, f32[16,24,256]{2,1,0:T(8,128)S(1)}, f32[1,24,256]{2,1,0:T(8,128)S(1...) custom-call(f32[3,16,16,256]{3,2,1,0:T(8,128)S(1)} %get-tuple-elemen, ...), custom_call_target="tpu_custom_call" | custom-call | flops 1000 | bytes 7225344 | tf_op jit(solution)/shard_map/pallas_call | solution.py:442
  45.6 1.7 %shard_map.75 = (f32[3,16,16,256]{3,2,1,0:T(8,128)}, f32[16,16,256]{2,1,0:T(8,128)}) custom-call(s32[2]{0:T(128)S(1)} %pad_add_fusion.parity, f32[3,16,16,256]{3,2,1,0:T(8,128)S(1)} %get-tuple-element.42.flux, f32[16,24,256]{2,1,0:T(8,128)S(1)} %get-tuple-element.43.own_c, f32[16,24,256]{2,1,0:T(8,128)S(1)} %get-tuple-element.44.own_scale, ...), custom_call_target="tpu_custom_call" | custom-call | flops 1000 | bytes 5365768 | tf_op jit(solution)/shard_map/pallas_call | solution.py:442
  (13 shorter events, 0.0 us)
Async XLA Ops:
  0.6 1.1 %copy-start = (f32[3,1,16,16,256]{4,3,2,1,0:T(8,128)S(1)}, f32[3,1,16,16,256]{4,3,2,1,0:T(8,128)}, u32[]{:S(2)}) copy-start(f32[3,1,16,16,256]{4,3,2,1,0:T(8,128)} %param.5) | copy-start | bytes 2359300
  1.8 5.0 %copy-start.1 = (f32[3,1,16,16,256]{4,3,2,1,0:T(8,128)S(1)}, f32[3,1,16,16,256]{4,3,2,1,0:T(8,128)}, u32[]{:S(2)}) copy-start(f32[3,1,16,16,256]{4,3,2,1,0:T(8,128)} %param.5) | copy-start | bytes 2359300
  1.8 5.0 %copy-start.2 = (f32[1,16,16,256]{3,2,1,0:T(8,128)S(1)}, f32[1,16,16,256]{3,2,1,0:T(8,128)}, u32[]{:S(2)}) copy-start(f32[1,16,16,256]{3,2,1,0:T(8,128)} %param.6) | copy-start | bytes 786436
  1.8 5.0 %copy-start.5 = (f32[3,16,16,256]{3,2,1,0:T(8,128)S(1)}, f32[3,16,16,256]{3,2,1,0:T(8,128)}, u32[]{:S(2)}) copy-start(f32[3,16,16,256]{3,2,1,0:T(8,128)} %visc.3) | copy-start | bytes 2359300
  1.9 17.6 %collective-permute-start = (f32[18,16,256]{2,1,0:T(8,128)S(1)}, f32[18,16,256]{2,1,0:T(8,128)S(1)}, u32[]{:S(2)}, u32[]{:S(2)}) collective-permute-start(f32[18,16,256]{2,1,0:T(8,128)S(1)} %shard_map.68), channel_id=1, source_target_pairs={{0,64},{64,128},{128,192},{192,256},{256,320},{320,384},{384,448},... | collective-permute-start | bytes 884744 | tf_op jit(solution)/shard_map/ppermute | solution.py:462
  6.8 12.6 %copy-start.4 = (f32[3,1,16,16,256]{4,3,2,1,0:T(8,128)S(1)}, f32[3,1,16,16,256]{4,3,2,1,0:T(8,128)}, u32[]{:S(2)}) copy-start(f32[3,1,16,16,256]{4,3,2,1,0:T(8,128)} %param.7) | copy-start | bytes 2359300
  7.4 13.7 %collective-permute-start.1 = (f32[7,16,256]{2,1,0:T(8,128)S(1)}, f32[7,16,256]{2,1,0:T(8,128)S(1)}, u32[]{:S(2)}, u32[]{:S(2)}) collective-permute-start(f32[7,16,256]{2,1,0:T(8,128)S(1)} %get-tuple-element.31), channel_id=1, source_target_pairs={{8,16},{16,8},{24,32},{32,24},{40,48},{48,40},{56,0},{0,56},{9,17}... | collective-permute-start | bytes 344072 | tf_op jit(solution)/shard_map/ppermute | solution.py:22
  17.5 3.6 %collective-permute-start.2 = (f32[7,16,256]{2,1,0:T(8,128)S(1)}, f32[7,16,256]{2,1,0:T(8,128)S(1)}, u32[]{:S(2)}, u32[]{:S(2)}) collective-permute-start(f32[7,16,256]{2,1,0:T(8,128)S(1)} %get-tuple-element.32), channel_id=1, source_target_pairs={{0,8},{8,0},{16,24},{24,16},{32,40},{40,32},{48,56},{56,48},{1,9},... | collective-permute-start | bytes 344072 | tf_op jit(solution)/shard_map/ppermute | solution.py:26
  19.4 1.6 %copy-start.3 = (f32[1,16,16,256]{3,2,1,0:T(8,128)S(1)}, f32[1,16,16,256]{3,2,1,0:T(8,128)}, u32[]{:S(2)}) copy-start(f32[1,16,16,256]{3,2,1,0:T(8,128)} %param.8) | copy-start | bytes 786436
  22.1 10.5 %collective-permute-start.4 = (f32[168,256]{1,0:T(8,128)S(1)}, f32[168,256]{1,0:T(8,128)S(1)}, u32[]{:S(2)}, u32[]{:S(2)}) collective-permute-start(f32[168,256]{1,0:T(8,128)S(1)} %get-tuple-element.36), channel_id=1, source_target_pairs={{1,2},{2,1},{3,4},{4,3},{5,6},{6,5},{7,0},{0,7},{9,10},{10,9},{11,... | collective-permute-start | bytes 516104 | tf_op jit(solution)/shard_map/ppermute | solution.py:22
  27.8 7.6 %collective-permute-start.5 = (f32[168,256]{1,0:T(8,128)S(1)}, f32[168,256]{1,0:T(8,128)S(1)}, u32[]{:S(2)}, u32[]{:S(2)}) collective-permute-start(f32[168,256]{1,0:T(8,128)S(1)} %get-tuple-element.37), channel_id=1, source_target_pairs={{0,1},{1,0},{2,3},{3,2},{4,5},{5,4},{6,7},{7,6},{8,9},{9,8},{10,11... | collective-permute-start | bytes 516104 | tf_op jit(solution)/shard_map/ppermute | solution.py:26
  29.8 14.6 %collective-permute-start.3 = (f32[488,256]{1,0:T(8,128)S(1)}, f32[488,256]{1,0:T(8,128)S(1)}, u32[]{:S(2)}, u32[]{:S(2)}) collective-permute-start(f32[488,256]{1,0:T(8,128)S(1)} %shard_map.72), channel_id=1, source_target_pairs={{0,64},{64,128},{128,192},{192,256},{256,320},{320,384},{384,448},... | collective-permute-start | bytes 1499144 | tf_op jit(solution)/shard_map/ppermute | solution.py:470
  36.1 9.5 %collective-permute-start.6 = (f32[3,24,256]{2,1,0:T(8,128)S(1)}, f32[3,24,256]{2,1,0:T(8,128)S(1)}, u32[]{:S(2)}, u32[]{:S(2)}) collective-permute-start(f32[3,24,256]{2,1,0:T(8,128)S(1)} %get-tuple-element.50), channel_id=1, source_target_pairs={{8,16},{16,8},{24,32},{32,24},{40,48},{48,40},{56,0},{0,56},{9,17}... | collective-permute-start | bytes 221192 | tf_op jit(solution)/shard_map/ppermute | solution.py:22
  39.5 6.2 %collective-permute-start.7 = (f32[3,24,256]{2,1,0:T(8,128)S(1)}, f32[3,24,256]{2,1,0:T(8,128)S(1)}, u32[]{:S(2)}, u32[]{:S(2)}) collective-permute-start(f32[3,24,256]{2,1,0:T(8,128)S(1)} %get-tuple-element.51), channel_id=1, source_target_pairs={{0,8},{8,0},{16,24},{24,16},{32,40},{40,32},{48,56},{56,48},{1,9},... | collective-permute-start | bytes 221192 | tf_op jit(solution)/shard_map/ppermute | solution.py:26

commit v4 on v3

--- a/solution.py
+++ b/solution.py
@@ -7,6 +7,7 @@
 
 RELAX = 1.5
 DAMPING = 0.8
+MORE = 3
 EXT = 24
 
 
@@ -26,6 +27,10 @@
     return lax.ppermute(x, axis, even_pairs(lax.axis_size(axis)))
 
 
+def is_even(axis):
+    return lax.rem(lax.axis_index(axis), 2) == 0
+
+
 def above_z(x):
     return pltpu.roll(x, x.shape[1] - 1, 1)
 
@@ -51,7 +56,7 @@
 
 
 def ring_plan(nx, ny):
-    layers = [(c, i) for c in range(3) for i in (0, 1, nx - 1)] + [(0, nx - 2)]
+    layers = [(c, i) for c in range(3) for i in (*range(2 + MORE), nx - 1)] + [(0, nx - 2)]
     whole = {key: tile for tile, key in enumerate(layers)}
     lines = [(0, 1, ny - 1), (0, 1, ny - 2, ny - 1), (0, 1, ny - 1)]
     single = {}
@@ -98,9 +103,9 @@
         ring[tile, row : row + 1, :] = v[c, i, j : j + 1, :]
 
 
-def face_kernel(parity, v, p, visc, send_odd, send_even):
+def face_kernel(v, p, visc, send_odd, send_even):
     nx = v.shape[1]
-    even_x = parity[0] == 0
+    even_x = is_even("gx")
 
     def send(layer, up, down):
         send_even[layer] = jnp.where(even_x, up, down)
@@ -143,16 +148,16 @@
             flux[c, i] = k * (f[c, i] + prev + nu * near - slope) + flow * (1.0 - 1.0 / RELAX)
 
 
-def edge_kernel(parity, flux0, coeff, v, p, s, got_odd, got_even, lo_x, hi_x, total, send_odd, send_even, own):
+def edge_kernel(flux0, coeff, v, p, s, got_odd, got_even, lo_x, hi_x, total, send_odd, send_even, own):
     nx, ny = s.shape[0], s.shape[1]
     shape = s.shape[1:]
     rows = row_id(shape)
     first = rows == 0
-    even_y = parity[1] == 0
+    even_y = is_even("gy")
     zero = jnp.zeros((1, shape[1]), jnp.float32)
     top, low, near = slice(ny - 1, ny), slice(0, 1), slice(1, 2)
     for layer in range(7):
-        lo_x[layer], hi_x[layer] = pick(parity[0] == 0, got_odd, got_even, layer)
+        lo_x[layer], hi_x[layer] = pick(is_even("gx"), got_odd, got_even, layer)
 
     def send(layer, i, up, down):
         row = layer * nx + i
@@ -259,11 +264,11 @@
 
 
 def strip_kernel(
-    parity, flux0, coeff, s, total, lo_x, hi_x, got_odd, got_even, own,
+    flux0, coeff, s, total, lo_x, hi_x, got_odd, got_even, own,
     lo_y, hi_y, out_rows, send_odd, send_even, right_x, scale_x, side,
 ):
     nx, ny = s.shape[0], s.shape[1]
-    even_x, even_y = parity[0] == 0, parity[1] == 0
+    even_x, even_y = is_even("gx"), is_even("gy")
     rows = row_id(s.shape[1:])
     first = rows == 0
     for layer in range(10):
@@ -366,7 +371,7 @@
 
 
 def last_kernel(
-    parity, flux, own_c, own_scale, side, own_kx, own_ky, own_kz, ends, p, lo_x, hi_x, got_odd, got_even, wide_v, wide_p,
+    flux, own_c, own_scale, side, own_kx, own_ky, own_kz, ends, p, lo_x, hi_x, got_odd, got_even, wide_v, wide_p,
     new_v, new_p, edge, low_v, low_p, top_v, top_p, top_x, sems,
 ):
     nx, ny = p.shape[0], p.shape[1]
@@ -378,7 +383,7 @@
     ]
     for copy in ready:
         copy.start()
-    even_x = parity[0] == 0
+    even_x = is_even("gx")
     lo0, hi0 = pick(even_x, got_odd, got_even, 0)
     lo1, hi1 = pick(even_x, got_odd, got_even, 1)
     _, hi2 = pick(even_x, got_odd, got_even, 2)
@@ -430,19 +435,18 @@
 
 
 VM = pl.BlockSpec(memory_space=pltpu.VMEM)
-SM = pl.BlockSpec(memory_space=pltpu.SMEM)
 
 
 ANY = pl.BlockSpec(memory_space=pl.ANY)
 
 
-def call(kernel, args, outs, scratch=(), scalars=True, flops=1000, far=0):
+def call(kernel, args, outs, scratch=(), flops=1000, far=0):
     shapes = [jax.ShapeDtypeStruct(s, jnp.float32) for s in outs]
     size = sum(4 * a.size for a in args) + sum(4 * s.size for s in shapes)
     return pl.pallas_call(
         kernel,
         out_shape=shapes,
-        in_specs=[SM] * scalars + [VM] * (len(args) - scalars),
+        in_specs=[VM] * len(args),
         out_specs=[VM] * (len(shapes) - far) + [ANY] * far,
         scratch_shapes=[pltpu.VMEM(s, jnp.float32) for s in scratch] + [pltpu.SemaphoreType.DMA((9,))] * (far > 0),
         compiler_params=pltpu.CompilerParams(vmem_limit_bytes=40 * 2**20),
@@ -455,23 +459,22 @@
     nx, ny, nz = p.shape
     steps = lax.axis_size("ta")
     ahead = [(i, i + 1) for i in range(steps - 1)]
-    parity = jnp.stack([lax.axis_index("gx") % 2, lax.axis_index("gy") % 2]).astype(jnp.int32)
-    (ring,) = call(ring_kernel, (v,), ((ring_plan(nx, ny)[3], ny, nz),), scalars=False, flops=20_000_000_000)
-    face_odd, face_even = call(face_kernel, (parity, v, p, viscosity), ((7, ny, nz), (7, ny, nz)), flops=20_000_000_000)
+    (ring,) = call(ring_kernel, (v,), ((ring_plan(nx, ny)[3], ny, nz),), flops=20_000_000_000)
+    face_odd, face_even = call(face_kernel, (v, p, viscosity), ((7, ny, nz), (7, ny, nz)), flops=20_000_000_000)
     odd_x, even_x = swap_odd(face_odd, "gx"), swap_even(face_even, "gx")
     ring = lax.ppermute(ring, "ta", ahead)
-    flux0, coeff = call(local_kernel, (v, p, f, viscosity, ring), (v.shape,) * 2, scalars=False)
+    flux0, coeff = call(local_kernel, (v, p, f, viscosity, ring), (v.shape,) * 2)
     lo_x, hi_x, total, send_odd, send_even, own = call(
         edge_kernel,
-        (parity, flux0, coeff, v, p, s, odd_x, even_x),
+        (flux0, coeff, v, p, s, odd_x, even_x),
         ((7, ny, nz), (7, ny, nz), p.shape, (10 * nx + 8, nz), (10 * nx + 8, nz), (8, nx, nz)),
     )
-    (bulk,) = call(bulk_kernel, (v, total), ((bulk_plan(nx, ny)[1], nz),), scalars=False)
+    (bulk,) = call(bulk_kernel, (v, total), ((bulk_plan(nx, ny)[1], nz),))
     prev = lax.ppermute(bulk, "ta", ahead)
     odd_y, even_y = swap_odd(send_odd, "gy"), swap_even(send_even, "gy")
     lo_y, hi_y, out_rows, send_odd, send_even = call(
         strip_kernel,
-        (parity, flux0, coeff, s, total, lo_x, hi_x, odd_y, even_y, own),
+        (flux0, coeff, s, total, lo_x, hi_x, odd_y, even_y, own),
         ((10, nx, nz), (10, nx, nz), (8, nx, nz), (3, EXT, nz), (3, EXT, nz)),
         ((3, EXT, nz), (3, EXT, nz), (1, EXT, nz)),
         flops=20_000_000_000,
@@ -483,11 +486,10 @@
         (v.shape, (nx, EXT, nz), (nx, EXT, nz), (1, EXT, nz))
         + ((nx, EXT, nz),) * 3
         + ((2, EXT, nz), (3, nx - 3, ny, nz), (nx - 3, ny, nz)),
-        scalars=False,
     )
     new_v, new_p = call(
         last_kernel,
-        (parity, flux, first_c, scale, side, kx, ky, kz, ends, p, lo_x, hi_x, odd_x, even_x, wide_v, wide_p),
+        (flux, first_c, scale, side, kx, ky, kz, ends, p, lo_x, hi_x, odd_x, even_x, wide_v, wide_p),
         (v.shape, p.shape),
         ((4, EXT, nz), (3, 2, ny, nz), (2, ny, nz), (3, 1, ny, nz), (1, ny, nz), (1, ny, nz)),
         far=2,

time: 47.7 us -> 44.9 us (0.941)
  the two profiles are of different devices: /device:TPU:24 before, /device:TPU:25 now
where the time goes in v4:
time: 44.9 us; the launch traced here: 44.5 us
  starting transfers between devices  36 us (80%)
  Pallas kernels  4 us (9%)
  waiting for transfers between devices  2.47 us (6%)
  local copies, waits for them, and re-layouts  1.17 us (3%)
  between operations  0.83 us (2%)
    ppermute x3, starting transfers between devices, swap_odd(): return lax.ppermute(x, axis, odd_pairs(lax.axis_size(axis)))  17.2 us
    ppermute x3, starting transfers between devices, swap_even(): return lax.ppermute(x, axis, even_pairs(lax.axis_size(axis)))  12 us
    ppermute x1, starting transfers between devices, body(): ring = lax.ppermute(ring, 'ta', ahead)  4.55 us
    pallas_call x8, Pallas kernels, call(): pl.pallas_call(kernel, out_shape=shapes, in_specs=[VM] * len(args), out_s...  4 us
    ppermute x3, waiting for transfers between devices, swap_even(): return lax.ppermute(x, axis, even_pairs(lax.axis_size(axis)))  2.46 us
    ppermute x1, starting transfers between devices, body(): prev = lax.ppermute(bulk, 'ta', ahead)  2.31 us
    unnamed x10, local copies, waits for them, and re-layouts  1.17 us
  transfers between devices with their start and end apart: 8, of which 2 were waited for; matrix products, arithmetic and copies ran while one was open for 0% of the time, Pallas kernels for 5%

profile of v4, /device:TPU:25, one launch (start us, length us, event | category | flops | bytes accessed | tf_op | source)
XLA Modules:
  0.0 44.5 jit_solution(18346172250527035065)
XLA Ops:
  0.6 1.1 %copy-done = f32[3,1,16,16,256]{4,3,2,1,0:T(8,128)S(1)} copy-done((f32[3,1,16,16,256]{4,3,2,1,0:T(8,128)S(1)}, f32[3,1,16,16,256]{4,3,2,1,0:T(8,128)}, u32[]{:S(2)}) %copy-start) | copy-done | bytes 786456
  1.8 0.1 shard_map.68
  1.8 4.5 %collective-permute-start = (f32[26,16,256]{2,1,0:T(8,128)S(1)}, f32[26,16,256]{2,1,0:T(8,128)S(1)}, u32[]{:S(2)}, u32[]{:S(2)}) collective-permute-start(f32[26,16,256]{2,1,0:T(8,128)S(1)} %shard_map.68), channel_id=1, source_target_pairs={{0,64},{64,128},{128,192},{192,256},{256,320},{320,384},{384,448},... | collective-permute-start | bytes 1277960 | tf_op jit(solution)/shard_map/ppermute | solution.py:465
  6.4 0.0 copy-start.3
  6.5 6.8 %collective-permute-start.1 = (f32[7,16,256]{2,1,0:T(8,128)S(1)}, f32[7,16,256]{2,1,0:T(8,128)S(1)}, u32[]{:S(2)}, u32[]{:S(2)}) collective-permute-start(f32[7,16,256]{2,1,0:T(8,128)S(1)} %get-tuple-element.31), channel_id=1, source_target_pairs={{8,16},{16,8},{24,32},{32,24},{40,48},{48,40},{56,0},{0,56},{9,17}... | collective-permute-start | bytes 344072 | tf_op jit(solution)/shard_map/ppermute | solution.py:23
  13.3 6.3 %collective-permute-start.2 = (f32[7,16,256]{2,1,0:T(8,128)S(1)}, f32[7,16,256]{2,1,0:T(8,128)S(1)}, u32[]{:S(2)}, u32[]{:S(2)}) collective-permute-start(f32[7,16,256]{2,1,0:T(8,128)S(1)} %get-tuple-element.32), channel_id=1, source_target_pairs={{0,8},{8,0},{16,24},{24,16},{32,40},{40,32},{48,56},{56,48},{1,9},... | collective-permute-start | bytes 344072 | tf_op jit(solution)/shard_map/ppermute | solution.py:27
  19.6 0.0 collective-permute-done.ring
  19.6 0.0 copy-start.2
  19.6 0.8 %shard_map.69 = (f32[3,16,16,256]{3,2,1,0:T(8,128)S(1)}, f32[3,16,16,256]{3,2,1,0:T(8,128)S(1)}) custom-call(f32[3,16,16,256]{3,2,1,0:T(8,128)S(1)} %bitcast.10, f32[16,16,256]{2,1,0:T(8,128)S(1)} %bitcast.14, f32[3,16,16,256]{3,2,1,0:T(8,128)S(1)} %bitcast.21, f32[3,16,16,256]{3,2,1,0:T(8,128)S(1)} %copy-done.4, f32[26,16,256]{2,1,0:T(8,128)S(1)} %collective-permute-done.ring), custom_call_target="tpu_custom_call" | custom-call | flops 1000 | bytes 4620288 | tf_op jit(solution)/shard_map/pallas_call | solution.py:446
  20.4 0.1 collective-permute-done.2.got_even
  20.5 0.0 copy-done.2
  20.6 0.5 %shard_map.71 = (f32[7,16,256]{2,1,0:T(8,128)S(1)}, f32[7,16,256]{2,1,0:T(8,128)S(1)}, f32[16,16,256]{2,1,0:T(8,128)S(1)}, f32[168,256]{1,0:T(8,128)S(1)}, f32[1...) custom-call(f32[3,16,16,256]{3,2,1,0:T(8,128)S(1)} %get-tuple-element.29.flux0, ...), custom_call_target="tpu_custom_call" | custom-call | flops 1000 | bytes 4079616 | tf_op jit(solution)/shard_map/pallas_call | solution.py:446
  21.1 5.3 %collective-permute-start.4 = (f32[168,256]{1,0:T(8,128)S(1)}, f32[168,256]{1,0:T(8,128)S(1)}, u32[]{:S(2)}, u32[]{:S(2)}) collective-permute-start(f32[168,256]{1,0:T(8,128)S(1)} %get-tuple-element.36), channel_id=1, source_target_pairs={{1,2},{2,1},{3,4},{4,3},{5,6},{6,5},{7,0},{0,7},{9,10},{10,9},{11,... | collective-permute-start | bytes 516104 | tf_op jit(solution)/shard_map/ppermute | solution.py:23
  26.4 1.9 %collective-permute-start.5 = (f32[168,256]{1,0:T(8,128)S(1)}, f32[168,256]{1,0:T(8,128)S(1)}, u32[]{:S(2)}, u32[]{:S(2)}) collective-permute-start(f32[168,256]{1,0:T(8,128)S(1)} %get-tuple-element.37), channel_id=1, source_target_pairs={{0,1},{1,0},{2,3},{3,2},{4,5},{5,4},{6,7},{7,6},{8,9},{9,8},{10,11... | collective-permute-start | bytes 516104 | tf_op jit(solution)/shard_map/ppermute | solution.py:27
  28.3 0.1 shard_map.72
  28.4 2.3 %collective-permute-start.3 = (f32[376,256]{1,0:T(8,128)S(1)}, f32[376,256]{1,0:T(8,128)S(1)}, u32[]{:S(2)}, u32[]{:S(2)}) collective-permute-start(f32[376,256]{1,0:T(8,128)S(1)} %shard_map.72), channel_id=1, source_target_pairs={{0,64},{64,128},{128,192},{192,256},{256,320},{320,384},{384,448},... | collective-permute-start | bytes 1155080 | tf_op jit(solution)/shard_map/ppermute | solution.py:473
  30.7 0.0 collective-permute-done.4.got_odd
  30.7 2.4 %collective-permute-done.5.got_even = f32[168,256]{1,0:T(8,128)S(1)} collective-permute-done((f32[168,256]{1,0:T(8,128)S(1)}, f32[168,256]{1,0:T(8,128)S(1)}, u32[]{:S(2)}, u32[]{:S(2)}) %collective-permute-start.5) | collective-permute-done | bytes 172064 | tf_op jit(solution)/shard_map/ppermute | solution.py:27
  33.1 0.2 shard_map.73
  33.2 5.1 %collective-permute-start.6 = (f32[3,24,256]{2,1,0:T(8,128)S(1)}, f32[3,24,256]{2,1,0:T(8,128)S(1)}, u32[]{:S(2)}, u32[]{:S(2)}) collective-permute-start(f32[3,24,256]{2,1,0:T(8,128)S(1)} %get-tuple-element.50), channel_id=1, source_target_pairs={{8,16},{16,8},{24,32},{32,24},{40,48},{48,40},{56,0},{0,56},{9,17}... | collective-permute-start | bytes 221192 | tf_op jit(solution)/shard_map/ppermute | solution.py:23
  38.3 3.8 %collective-permute-start.7 = (f32[3,24,256]{2,1,0:T(8,128)S(1)}, f32[3,24,256]{2,1,0:T(8,128)S(1)}, u32[]{:S(2)}, u32[]{:S(2)}) collective-permute-start(f32[3,24,256]{2,1,0:T(8,128)S(1)} %get-tuple-element.51), channel_id=1, source_target_pairs={{0,8},{8,0},{16,24},{24,16},{32,40},{40,32},{48,56},{56,48},{1,9},... | collective-permute-start | bytes 221192 | tf_op jit(solution)/shard_map/ppermute | solution.py:27
  42.1 1.2 %shard_map.74 = (f32[3,16,16,256]{3,2,1,0:T(8,128)S(1)}, f32[16,24,256]{2,1,0:T(8,128)S(1)}, f32[16,24,256]{2,1,0:T(8,128)S(1)}, f32[1,24,256]{2,1,0:T(8,128)S(1...) custom-call(f32[3,16,16,256]{3,2,1,0:T(8,128)S(1)} %get-tuple-elemen, ...), custom_call_target="tpu_custom_call" | custom-call | flops 1000 | bytes 7110656 | tf_op jit(solution)/shard_map/pallas_call | solution.py:446
  43.3 0.0 collective-permute-done.7.got_even
  43.3 1.2 %shard_map.75 = (f32[3,16,16,256]{3,2,1,0:T(8,128)}, f32[16,16,256]{2,1,0:T(8,128)}) custom-call(f32[3,16,16,256]{3,2,1,0:T(8,128)S(1)} %get-tuple-element.42.flux, f32[16,24,256]{2,1,0:T(8,128)S(1)} %get-tuple-element.43.own_c, f32[16,24,256]{2,1,0:T(8,128)S(1)} %get-tuple-element.44.own_scale, f32[1,24,256]{2,1,0:T(8,128)S(1)} %get-tuple-element.45.side, ...), custom_call_target="tpu_custom_call" | custom-call | flops 1000 | bytes 5365760 | tf_op jit(solution)/shard_map/pallas_call | solution.py:446
  (10 shorter events, 0.1 us)
Async XLA Ops:
  0.6 1.1 %copy-start = (f32[3,1,16,16,256]{4,3,2,1,0:T(8,128)S(1)}, f32[3,1,16,16,256]{4,3,2,1,0:T(8,128)}, u32[]{:S(2)}) copy-start(f32[3,1,16,16,256]{4,3,2,1,0:T(8,128)} %param.5) | copy-start | bytes 2359300
  1.8 4.6 %copy-start.1 = (f32[1,16,16,256]{3,2,1,0:T(8,128)S(1)}, f32[1,16,16,256]{3,2,1,0:T(8,128)}, u32[]{:S(2)}) copy-start(f32[1,16,16,256]{3,2,1,0:T(8,128)} %param.6) | copy-start | bytes 786436
  1.8 4.6 %copy-start.4 = (f32[3,16,16,256]{3,2,1,0:T(8,128)S(1)}, f32[3,16,16,256]{3,2,1,0:T(8,128)}, u32[]{:S(2)}) copy-start(f32[3,16,16,256]{3,2,1,0:T(8,128)} %visc.3) | copy-start | bytes 2359300
  1.8 17.7 %collective-permute-start = (f32[26,16,256]{2,1,0:T(8,128)S(1)}, f32[26,16,256]{2,1,0:T(8,128)S(1)}, u32[]{:S(2)}, u32[]{:S(2)}) collective-permute-start(f32[26,16,256]{2,1,0:T(8,128)S(1)} %shard_map.68), channel_id=1, source_target_pairs={{0,64},{64,128},{128,192},{192,256},{256,320},{320,384},{384,448},... | collective-permute-start | bytes 1277960 | tf_op jit(solution)/shard_map/ppermute | solution.py:465
  6.4 13.2 %copy-start.3 = (f32[3,1,16,16,256]{4,3,2,1,0:T(8,128)S(1)}, f32[3,1,16,16,256]{4,3,2,1,0:T(8,128)}, u32[]{:S(2)}) copy-start(f32[3,1,16,16,256]{4,3,2,1,0:T(8,128)} %param.7) | copy-start | bytes 2359300
  6.5 14.0 %collective-permute-start.1 = (f32[7,16,256]{2,1,0:T(8,128)S(1)}, f32[7,16,256]{2,1,0:T(8,128)S(1)}, u32[]{:S(2)}, u32[]{:S(2)}) collective-permute-start(f32[7,16,256]{2,1,0:T(8,128)S(1)} %get-tuple-element.31), channel_id=1, source_target_pairs={{8,16},{16,8},{24,32},{32,24},{40,48},{48,40},{56,0},{0,56},{9,17}... | collective-permute-start | bytes 344072 | tf_op jit(solution)/shard_map/ppermute | solution.py:23
  13.3 7.3 %collective-permute-start.2 = (f32[7,16,256]{2,1,0:T(8,128)S(1)}, f32[7,16,256]{2,1,0:T(8,128)S(1)}, u32[]{:S(2)}, u32[]{:S(2)}) collective-permute-start(f32[7,16,256]{2,1,0:T(8,128)S(1)} %get-tuple-element.32), channel_id=1, source_target_pairs={{0,8},{8,0},{16,24},{24,16},{32,40},{40,32},{48,56},{56,48},{1,9},... | collective-permute-start | bytes 344072 | tf_op jit(solution)/shard_map/ppermute | solution.py:27
  19.6 1.0 %copy-start.2 = (f32[1,16,16,256]{3,2,1,0:T(8,128)S(1)}, f32[1,16,16,256]{3,2,1,0:T(8,128)}, u32[]{:S(2)}) copy-start(f32[1,16,16,256]{3,2,1,0:T(8,128)} %param.8) | copy-start | bytes 786436
  21.1 9.6 %collective-permute-start.4 = (f32[168,256]{1,0:T(8,128)S(1)}, f32[168,256]{1,0:T(8,128)S(1)}, u32[]{:S(2)}, u32[]{:S(2)}) collective-permute-start(f32[168,256]{1,0:T(8,128)S(1)} %get-tuple-element.36), channel_id=1, source_target_pairs={{1,2},{2,1},{3,4},{4,3},{5,6},{6,5},{7,0},{0,7},{9,10},{10,9},{11,... | collective-permute-start | bytes 516104 | tf_op jit(solution)/shard_map/ppermute | solution.py:23
  26.4 6.7 %collective-permute-start.5 = (f32[168,256]{1,0:T(8,128)S(1)}, f32[168,256]{1,0:T(8,128)S(1)}, u32[]{:S(2)}, u32[]{:S(2)}) collective-permute-start(f32[168,256]{1,0:T(8,128)S(1)} %get-tuple-element.37), channel_id=1, source_target_pairs={{0,1},{1,0},{2,3},{3,2},{4,5},{5,4},{6,7},{7,6},{8,9},{9,8},{10,11... | collective-permute-start | bytes 516104 | tf_op jit(solution)/shard_map/ppermute | solution.py:27
  28.4 13.7 %collective-permute-start.3 = (f32[376,256]{1,0:T(8,128)S(1)}, f32[376,256]{1,0:T(8,128)S(1)}, u32[]{:S(2)}, u32[]{:S(2)}) collective-permute-start(f32[376,256]{1,0:T(8,128)S(1)} %shard_map.72), channel_id=1, source_target_pairs={{0,64},{64,128},{128,192},{192,256},{256,320},{320,384},{384,448},... | collective-permute-start | bytes 1155080 | tf_op jit(solution)/shard_map/ppermute | solution.py:473
  33.2 10.1 %collective-permute-start.6 = (f32[3,24,256]{2,1,0:T(8,128)S(1)}, f32[3,24,256]{2,1,0:T(8,128)S(1)}, u32[]{:S(2)}, u32[]{:S(2)}) collective-permute-start(f32[3,24,256]{2,1,0:T(8,128)S(1)} %get-tuple-element.50), channel_id=1, source_target_pairs={{8,16},{16,8},{24,32},{32,24},{40,48},{48,40},{56,0},{0,56},{9,17}... | collective-permute-start | bytes 221192 | tf_op jit(solution)/shard_map/ppermute | solution.py:23
  38.3 5.0 %collective-permute-start.7 = (f32[3,24,256]{2,1,0:T(8,128)S(1)}, f32[3,24,256]{2,1,0:T(8,128)S(1)}, u32[]{:S(2)}, u32[]{:S(2)}) collective-permute-start(f32[3,24,256]{2,1,0:T(8,128)S(1)} %get-tuple-element.51), channel_id=1, source_target_pairs={{0,8},{8,0},{16,24},{24,16},{32,40},{40,32},{48,56},{56,48},{1,9},... | collective-permute-start | bytes 221192 | tf_op jit(solution)/shard_map/ppermute | solution.py:27

commit v5 on v4

--- a/solution.py
+++ b/solution.py
@@ -7,7 +7,7 @@
 
 RELAX = 1.5
 DAMPING = 0.8
-MORE = 3
+MORE = 2
 EXT = 24
 
 
@@ -296,9 +296,8 @@
     out_rows[6] = hi_y[9]
     side_16, side_17 = hi_few[0:1] + edge[nx - 1 :], hi_few[1:2]
 
-    right_x[...] = jnp.zeros_like(right_x)
-    scale_x[...] = jnp.zeros_like(scale_x)
-    side[...] = jnp.zeros_like(side)
+    for ref in (right_x, scale_x, side):
+        ref[:, ny:, :] = jnp.zeros((ref.shape[0], EXT - ny, ref.shape[2]), jnp.float32)
     args = (flux0, coeff, None, lo_x, hi_x, lo_y, hi_y, rows)
     before = None
     for n, i in enumerate((0, 1, nx - 1)):
@@ -342,7 +341,7 @@
     args = (flux0, coeff, prev, lo_x, hi_x, lo_y, hi_y, rows)
     zero = jnp.zeros((1, s.shape[2]), jnp.float32)
     for ref in (first_c, scale_x, side, kx, ky, kz):
-        ref[...] = jnp.zeros_like(ref)
+        ref[:, ny:, :] = jnp.zeros((ref.shape[0], EXT - ny, ref.shape[2]), jnp.float32)
     before = None
     for i in range(nx):
         row = slice(i, i + 1)
@@ -418,19 +417,23 @@
     for n, i in enumerate((0, 1)):
         low_v[0, n], low_v[1, n], low_v[2, n] = step_x(i), step_y(i), step_z(i)
         low_p[n] = p[i] + second[i][:ny]
+    low = [
+        pltpu.make_async_copy(low_v, new_v.at[:, pl.ds(0, 2)], sems.at[0]),
+        pltpu.make_async_copy(low_p, new_p.at[pl.ds(0, 2)], sems.at[1]),
+    ]
+    for copy in low:
+        copy.start()
     top_v[0, 0], top_v[1, 0], top_v[2, 0] = step_x(nx - 1), step_y(nx - 1), step_z(nx - 1)
     top_p[0] = p[nx - 1] + second[nx - 1][:ny]
     top_x[0] = step_x(nx - 2)
-    copies = [
-        pltpu.make_async_copy(low_v, new_v.at[:, pl.ds(0, 2)], sems.at[0]),
-        pltpu.make_async_copy(top_v, new_v.at[:, pl.ds(nx - 1, 1)], sems.at[1]),
-        pltpu.make_async_copy(top_x, new_v.at[0, pl.ds(nx - 2, 1)], sems.at[2]),
-        pltpu.make_async_copy(low_p, new_p.at[pl.ds(0, 2)], sems.at[3]),
+    top = [
+        pltpu.make_async_copy(top_v, new_v.at[:, pl.ds(nx - 1, 1)], sems.at[2]),
+        pltpu.make_async_copy(top_x, new_v.at[0, pl.ds(nx - 2, 1)], sems.at[3]),
         pltpu.make_async_copy(top_p, new_p.at[pl.ds(nx - 1, 1)], sems.at[4]),
     ]
-    for copy in copies:
+    for copy in top:
         copy.start()
-    for copy in ready + copies:
+    for copy in ready + low + top:
         copy.wait()
 
 

time: 44.9 us -> 44.8 us (level)
  the two profiles are of different devices: /device:TPU:25 before, /device:TPU:27 now
where the time goes in v5:
time: 44.8 us; the launch traced here: 44.4 us
  starting transfers between devices  35.1 us (78%)
  Pallas kernels  4.07 us (9%)
  waiting for transfers between devices  3.21 us (7%)
  local copies, waits for them, and re-layouts  1.17 us (3%)
  between operations  0.83 us (2%)
    ppermute x3, starting transfers between devices, swap_odd(): return lax.ppermute(x, axis, odd_pairs(lax.axis_size(axis)))  14.5 us
    ppermute x3, starting transfers between devices, swap_even(): return lax.ppermute(x, axis, even_pairs(lax.axis_size(axis)))  13.8 us
    ppermute x1, starting transfers between devices, body(): ring = lax.ppermute(ring, 'ta', ahead)  4.55 us
    pallas_call x8, Pallas kernels, call(): pl.pallas_call(kernel, out_shape=shapes, in_specs=[VM] * len(args), out_s...  4.07 us
    ppermute x3, waiting for transfers between devices, swap_even(): return lax.ppermute(x, axis, even_pairs(lax.axis_size(axis)))  3.2 us
    ppermute x1, starting transfers between devices, body(): prev = lax.ppermute(bulk, 'ta', ahead)  2.31 us
    unnamed x10, local copies, waits for them, and re-layouts  1.17 us
  transfers between devices with their start and end apart: 8, of which 2 were waited for; matrix products, arithmetic and copies ran while one was open for 0% of the time, Pallas kernels for 5%

profile of v5, /device:TPU:27, one launch (start us, length us, event | category | flops | bytes accessed | tf_op | source)
XLA Modules:
  0.0 44.4 jit_solution(1596783940459054503)
XLA Ops:
  0.6 1.1 %copy-done = f32[3,1,16,16,256]{4,3,2,1,0:T(8,128)S(1)} copy-done((f32[3,1,16,16,256]{4,3,2,1,0:T(8,128)S(1)}, f32[3,1,16,16,256]{4,3,2,1,0:T(8,128)}, u32[]{:S(2)}) %copy-start) | copy-done | bytes 786456
  1.8 0.1 shard_map.68
  1.8 4.5 %collective-permute-start = (f32[23,16,256]{2,1,0:T(8,128)S(1)}, f32[23,16,256]{2,1,0:T(8,128)S(1)}, u32[]{:S(2)}, u32[]{:S(2)}) collective-permute-start(f32[23,16,256]{2,1,0:T(8,128)S(1)} %shard_map.68), channel_id=1, source_target_pairs={{0,64},{64,128},{128,192},{192,256},{256,320},{320,384},{384,448},... | collective-permute-start | bytes 1130504 | tf_op jit(solution)/shard_map/ppermute | solution.py:468
  6.4 0.0 copy-start.3
  6.5 6.8 %collective-permute-start.1 = (f32[7,16,256]{2,1,0:T(8,128)S(1)}, f32[7,16,256]{2,1,0:T(8,128)S(1)}, u32[]{:S(2)}, u32[]{:S(2)}) collective-permute-start(f32[7,16,256]{2,1,0:T(8,128)S(1)} %get-tuple-element.31), channel_id=1, source_target_pairs={{8,16},{16,8},{24,32},{32,24},{40,48},{48,40},{56,0},{0,56},{9,17}... | collective-permute-start | bytes 344072 | tf_op jit(solution)/shard_map/ppermute | solution.py:23
  13.3 6.3 %collective-permute-start.2 = (f32[7,16,256]{2,1,0:T(8,128)S(1)}, f32[7,16,256]{2,1,0:T(8,128)S(1)}, u32[]{:S(2)}, u32[]{:S(2)}) collective-permute-start(f32[7,16,256]{2,1,0:T(8,128)S(1)} %get-tuple-element.32), channel_id=1, source_target_pairs={{0,8},{8,0},{16,24},{24,16},{32,40},{40,32},{48,56},{56,48},{1,9},... | collective-permute-start | bytes 344072 | tf_op jit(solution)/shard_map/ppermute | solution.py:27
  19.6 0.0 collective-permute-done.ring
  19.6 0.0 copy-start.2
  19.6 0.8 %shard_map.69 = (f32[3,16,16,256]{3,2,1,0:T(8,128)S(1)}, f32[3,16,16,256]{3,2,1,0:T(8,128)S(1)}) custom-call(f32[3,16,16,256]{3,2,1,0:T(8,128)S(1)} %bitcast.10, f32[16,16,256]{2,1,0:T(8,128)S(1)} %bitcast.14, f32[3,16,16,256]{3,2,1,0:T(8,128)S(1)} %bitcast.21, f32[3,16,16,256]{3,2,1,0:T(8,128)S(1)} %copy-done.4, f32[23,16,256]{2,1,0:T(8,128)S(1)} %collective-permute-done.ring), custom_call_target="tpu_custom_call" | custom-call | flops 1000 | bytes 4571136 | tf_op jit(solution)/shard_map/pallas_call | solution.py:449
  20.5 0.0 collective-permute-done.1.got_odd
  20.5 0.1 collective-permute-done.2.got_even
  20.5 0.0 copy-done.2
  20.6 0.5 %shard_map.71 = (f32[7,16,256]{2,1,0:T(8,128)S(1)}, f32[7,16,256]{2,1,0:T(8,128)S(1)}, f32[16,16,256]{2,1,0:T(8,128)S(1)}, f32[168,256]{1,0:T(8,128)S(1)}, f32[1...) custom-call(f32[3,16,16,256]{3,2,1,0:T(8,128)S(1)} %get-tuple-element.29.flux0, ...), custom_call_target="tpu_custom_call" | custom-call | flops 1000 | bytes 4079616 | tf_op jit(solution)/shard_map/pallas_call | solution.py:449
  21.1 3.1 %collective-permute-start.4 = (f32[168,256]{1,0:T(8,128)S(1)}, f32[168,256]{1,0:T(8,128)S(1)}, u32[]{:S(2)}, u32[]{:S(2)}) collective-permute-start(f32[168,256]{1,0:T(8,128)S(1)} %get-tuple-element.36), channel_id=1, source_target_pairs={{1,2},{2,1},{3,4},{4,3},{5,6},{6,5},{7,0},{0,7},{9,10},{10,9},{11,... | collective-permute-start | bytes 516104 | tf_op jit(solution)/shard_map/ppermute | solution.py:23
  24.2 3.1 %collective-permute-start.5 = (f32[168,256]{1,0:T(8,128)S(1)}, f32[168,256]{1,0:T(8,128)S(1)}, u32[]{:S(2)}, u32[]{:S(2)}) collective-permute-start(f32[168,256]{1,0:T(8,128)S(1)} %get-tuple-element.37), channel_id=1, source_target_pairs={{0,1},{1,0},{2,3},{3,2},{4,5},{5,4},{6,7},{7,6},{8,9},{9,8},{10,11... | collective-permute-start | bytes 516104 | tf_op jit(solution)/shard_map/ppermute | solution.py:27
  27.3 0.1 shard_map.72
  27.4 2.3 %collective-permute-start.3 = (f32[416,256]{1,0:T(8,128)S(1)}, f32[416,256]{1,0:T(8,128)S(1)}, u32[]{:S(2)}, u32[]{:S(2)}) collective-permute-start(f32[416,256]{1,0:T(8,128)S(1)} %shard_map.72), channel_id=1, source_target_pairs={{0,64},{64,128},{128,192},{192,256},{256,320},{320,384},{384,448},... | collective-permute-start | bytes 1277960 | tf_op jit(solution)/shard_map/ppermute | solution.py:476
  29.7 3.1 %collective-permute-done.5.got_even = f32[168,256]{1,0:T(8,128)S(1)} collective-permute-done((f32[168,256]{1,0:T(8,128)S(1)}, f32[168,256]{1,0:T(8,128)S(1)}, u32[]{:S(2)}, u32[]{:S(2)}) %collective-permute-start.5) | collective-permute-done | bytes 172064 | tf_op jit(solution)/shard_map/ppermute | solution.py:27
  32.9 0.2 shard_map.73
  33.0 4.6 %collective-permute-start.6 = (f32[3,24,256]{2,1,0:T(8,128)S(1)}, f32[3,24,256]{2,1,0:T(8,128)S(1)}, u32[]{:S(2)}, u32[]{:S(2)}) collective-permute-start(f32[3,24,256]{2,1,0:T(8,128)S(1)} %get-tuple-element.50), channel_id=1, source_target_pairs={{8,16},{16,8},{24,32},{32,24},{40,48},{48,40},{56,0},{0,56},{9,17}... | collective-permute-start | bytes 221192 | tf_op jit(solution)/shard_map/ppermute | solution.py:23
  37.7 4.3 %collective-permute-start.7 = (f32[3,24,256]{2,1,0:T(8,128)S(1)}, f32[3,24,256]{2,1,0:T(8,128)S(1)}, u32[]{:S(2)}, u32[]{:S(2)}) collective-permute-start(f32[3,24,256]{2,1,0:T(8,128)S(1)} %get-tuple-element.51), channel_id=1, source_target_pairs={{0,8},{8,0},{16,24},{24,16},{32,40},{40,32},{48,56},{56,48},{1,9},... | collective-permute-start | bytes 221192 | tf_op jit(solution)/shard_map/ppermute | solution.py:27
  42.0 1.2 %shard_map.74 = (f32[3,16,16,256]{3,2,1,0:T(8,128)S(1)}, f32[16,24,256]{2,1,0:T(8,128)S(1)}, f32[16,24,256]{2,1,0:T(8,128)S(1)}, f32[1,24,256]{2,1,0:T(8,128)S(1...) custom-call(f32[3,16,16,256]{3,2,1,0:T(8,128)S(1)} %get-tuple-elemen, ...), custom_call_target="tpu_custom_call" | custom-call | flops 1000 | bytes 7151616 | tf_op jit(solution)/shard_map/pallas_call | solution.py:449
  43.2 0.0 collective-permute-done.6.got_odd
  43.2 1.2 %shard_map.75 = (f32[3,16,16,256]{3,2,1,0:T(8,128)}, f32[16,16,256]{2,1,0:T(8,128)}) custom-call(f32[3,16,16,256]{3,2,1,0:T(8,128)S(1)} %get-tuple-element.42.flux, f32[16,24,256]{2,1,0:T(8,128)S(1)} %get-tuple-element.43.own_c, f32[16,24,256]{2,1,0:T(8,128)S(1)} %get-tuple-element.44.own_scale, f32[1,24,256]{2,1,0:T(8,128)S(1)} %get-tuple-element.45.side, ...), custom_call_target="tpu_custom_call" | custom-call | flops 1000 | bytes 5365760 | tf_op jit(solution)/shard_map/pallas_call | solution.py:449
  (10 shorter events, 0.1 us)
Async XLA Ops:
  0.6 1.1 %copy-start = (f32[3,1,16,16,256]{4,3,2,1,0:T(8,128)S(1)}, f32[3,1,16,16,256]{4,3,2,1,0:T(8,128)}, u32[]{:S(2)}) copy-start(f32[3,1,16,16,256]{4,3,2,1,0:T(8,128)} %param.5) | copy-start | bytes 2359300
  1.8 4.6 %copy-start.1 = (f32[1,16,16,256]{3,2,1,0:T(8,128)S(1)}, f32[1,16,16,256]{3,2,1,0:T(8,128)}, u32[]{:S(2)}) copy-start(f32[1,16,16,256]{3,2,1,0:T(8,128)} %param.6) | copy-start | bytes 786436
  1.8 4.6 %copy-start.4 = (f32[3,16,16,256]{3,2,1,0:T(8,128)S(1)}, f32[3,16,16,256]{3,2,1,0:T(8,128)}, u32[]{:S(2)}) copy-start(f32[3,16,16,256]{3,2,1,0:T(8,128)} %visc.3) | copy-start | bytes 2359300
  1.8 17.7 %collective-permute-start = (f32[23,16,256]{2,1,0:T(8,128)S(1)}, f32[23,16,256]{2,1,0:T(8,128)S(1)}, u32[]{:S(2)}, u32[]{:S(2)}) collective-permute-start(f32[23,16,256]{2,1,0:T(8,128)S(1)} %shard_map.68), channel_id=1, source_target_pairs={{0,64},{64,128},{128,192},{192,256},{256,320},{320,384},{384,448},... | collective-permute-start | bytes 1130504 | tf_op jit(solution)/shard_map/ppermute | solution.py:468
  6.4 13.2 %copy-start.3 = (f32[3,1,16,16,256]{4,3,2,1,0:T(8,128)S(1)}, f32[3,1,16,16,256]{4,3,2,1,0:T(8,128)}, u32[]{:S(2)}) copy-start(f32[3,1,16,16,256]{4,3,2,1,0:T(8,128)} %param.7) | copy-start | bytes 2359300
  6.5 14.0 %collective-permute-start.1 = (f32[7,16,256]{2,1,0:T(8,128)S(1)}, f32[7,16,256]{2,1,0:T(8,128)S(1)}, u32[]{:S(2)}, u32[]{:S(2)}) collective-permute-start(f32[7,16,256]{2,1,0:T(8,128)S(1)} %get-tuple-element.31), channel_id=1, source_target_pairs={{8,16},{16,8},{24,32},{32,24},{40,48},{48,40},{56,0},{0,56},{9,17}... | collective-permute-start | bytes 344072 | tf_op jit(solution)/shard_map/ppermute | solution.py:23
  13.3 7.3 %collective-permute-start.2 = (f32[7,16,256]{2,1,0:T(8,128)S(1)}, f32[7,16,256]{2,1,0:T(8,128)S(1)}, u32[]{:S(2)}, u32[]{:S(2)}) collective-permute-start(f32[7,16,256]{2,1,0:T(8,128)S(1)} %get-tuple-element.32), channel_id=1, source_target_pairs={{0,8},{8,0},{16,24},{24,16},{32,40},{40,32},{48,56},{56,48},{1,9},... | collective-permute-start | bytes 344072 | tf_op jit(solution)/shard_map/ppermute | solution.py:27
  19.6 1.0 %copy-start.2 = (f32[1,16,16,256]{3,2,1,0:T(8,128)S(1)}, f32[1,16,16,256]{3,2,1,0:T(8,128)}, u32[]{:S(2)}) copy-start(f32[1,16,16,256]{3,2,1,0:T(8,128)} %param.8) | copy-start | bytes 786436
  21.1 8.6 %collective-permute-start.4 = (f32[168,256]{1,0:T(8,128)S(1)}, f32[168,256]{1,0:T(8,128)S(1)}, u32[]{:S(2)}, u32[]{:S(2)}) collective-permute-start(f32[168,256]{1,0:T(8,128)S(1)} %get-tuple-element.36), channel_id=1, source_target_pairs={{1,2},{2,1},{3,4},{4,3},{5,6},{6,5},{7,0},{0,7},{9,10},{10,9},{11,... | collective-permute-start | bytes 516104 | tf_op jit(solution)/shard_map/ppermute | solution.py:23
  24.2 8.7 %collective-permute-start.5 = (f32[168,256]{1,0:T(8,128)S(1)}, f32[168,256]{1,0:T(8,128)S(1)}, u32[]{:S(2)}, u32[]{:S(2)}) collective-permute-start(f32[168,256]{1,0:T(8,128)S(1)} %get-tuple-element.37), channel_id=1, source_target_pairs={{0,1},{1,0},{2,3},{3,2},{4,5},{5,4},{6,7},{7,6},{8,9},{9,8},{10,11... | collective-permute-start | bytes 516104 | tf_op jit(solution)/shard_map/ppermute | solution.py:27
  27.4 14.6 %collective-permute-start.3 = (f32[416,256]{1,0:T(8,128)S(1)}, f32[416,256]{1,0:T(8,128)S(1)}, u32[]{:S(2)}, u32[]{:S(2)}) collective-permute-start(f32[416,256]{1,0:T(8,128)S(1)} %shard_map.72), channel_id=1, source_target_pairs={{0,64},{64,128},{128,192},{192,256},{256,320},{320,384},{384,448},... | collective-permute-start | bytes 1277960 | tf_op jit(solution)/shard_map/ppermute | solution.py:476
  33.0 10.2 %collective-permute-start.6 = (f32[3,24,256]{2,1,0:T(8,128)S(1)}, f32[3,24,256]{2,1,0:T(8,128)S(1)}, u32[]{:S(2)}, u32[]{:S(2)}) collective-permute-start(f32[3,24,256]{2,1,0:T(8,128)S(1)} %get-tuple-element.50), channel_id=1, source_target_pairs={{8,16},{16,8},{24,32},{32,24},{40,48},{48,40},{56,0},{0,56},{9,17}... | collective-permute-start | bytes 221192 | tf_op jit(solution)/shard_map/ppermute | solution.py:23
  37.7 5.5 %collective-permute-start.7 = (f32[3,24,256]{2,1,0:T(8,128)S(1)}, f32[3,24,256]{2,1,0:T(8,128)S(1)}, u32[]{:S(2)}, u32[]{:S(2)}) collective-permute-start(f32[3,24,256]{2,1,0:T(8,128)S(1)} %get-tuple-element.51), channel_id=1, source_target_pairs={{0,8},{8,0},{16,24},{24,16},{32,40},{40,32},{48,56},{56,48},{1,9},... | collective-permute-start | bytes 221192 | tf_op jit(solution)/shard_map/ppermute | solution.py:27
